TPU v7x, 32 devices: a whole 2x2x4 slice. The times are simulated.
32 devices in a mesh: dp: 4 (over z), ctx: 4 (over x, core), tp: 2 (over y).
Axes of the slice: x: 2, y: 2, z: 4, core: 2. Of those that a mesh axis runs over, the one named last changes fastest.
Arguments:
- hidden_in: bfloat16 [8192, 1024], P(('dp', 'ctx')), may hold values from -6 to 6
- out_grad: bfloat16 [8192, 1024], P(('dp', 'ctx')), may hold values from -6 to 6
- segments: int32 [4, 2048], P('dp', 'ctx'), may hold values from 0 to 3, never falling along the last dimension, each value on 1 to 1024 neighbouring positions
- routes: int32 [8192, 2], P(('dp', 'ctx')), may hold values from 0 to 3, all different within a row
- bucket_table: int32 [4095], replicated, may hold values from 0 to 31
- qkv_weight: bfloat16 [1024, 3, 1024], P(('dp', 'ctx'), None, 'tp'), may hold values from -0.1875 to 0.1875
- out_weight: bfloat16 [1024, 1024], P('tp', ('dp', 'ctx')), may hold values from -4 to 4
- router: bfloat16 [1024, 4], P(('dp', 'ctx')), may hold values from -0.1875 to 0.1875
- norm_gains: bfloat16 [2, 1024], P(None, ('dp', 'ctx')), may hold values from 0.5 to 1.5
- position_bias: float32 [16, 32], P('tp'), may hold values from -6 to 6
- expert_in: bfloat16 [4, 2, 1024, 2816], P('dp', None, 'ctx', 'tp'), may hold values from -0.1875 to 0.1875
- expert_down: bfloat16 [4, 2816, 1024], P('dp', 'tp', 'ctx'), may hold values from -0.875 to 0.875
- qkv_first: float32 [1024, 3, 1024], P(('dp', 'ctx'), None, 'tp'), may hold values from -192 to 192
- qkv_second: float32 [1024, 3, 1024], P(('dp', 'ctx'), None, 'tp'), may hold values from 3907.584 to 15482.88
- out_first: float32 [1024, 1024], P('tp', ('dp', 'ctx')), may hold values from -8 to 8
- out_second: float32 [1024, 1024], P('tp', ('dp', 'ctx')), may hold values from 7.632 to 30.24
- router_first: float32 [1024, 4], P(('dp', 'ctx')), may hold values from -2048 to 2048
- router_second: float32 [1024, 4], P(('dp', 'ctx')), may hold values from 640218.56 to 2536715
- gains_first: float32 [2, 1024], P(None, ('dp', 'ctx')), may hold values from -192 to 192
- gains_second: float32 [2, 1024], P(None, ('dp', 'ctx')), may hold values from 4220.191 to 16721.51
- bias_first: float32 [16, 32], P('tp'), may hold values from -128 to 128
- bias_second: float32 [16, 32], P('tp'), may hold values from 1953.792 to 7741.44
- in_first: float32 [4, 2, 1024, 2816], P('dp', None, 'ctx', 'tp'), may hold values from -32 to 32
- in_second: float32 [4, 2, 1024, 2816], P('dp', None, 'ctx', 'tp'), may hold values from 113.67517 to 450.41104
- down_first: float32 [4, 2816, 1024], P('dp', 'tp', 'ctx'), may hold values from -6 to 6
- down_second: float32 [4, 2816, 1024], P('dp', 'tp', 'ctx'), may hold values from 4.88448 to 19.3536
Outputs:
- output: float32 [8192, 1024], P(('dp', 'ctx'))
- input_grad: float32 [8192, 1024], P(('dp', 'ctx'))
- qkv_grad: float32 [1024, 3, 1024], P(('dp', 'ctx'), None, 'tp')
- qkv_first_new: float32 [1024, 3, 1024], P(('dp', 'ctx'), None, 'tp')
- qkv_second_new: float32 [1024, 3, 1024], P(('dp', 'ctx'), None, 'tp')
- qkv_update: float32 [1024, 3, 1024], P(('dp', 'ctx'), None, 'tp')
- out_grad_weight: float32 [1024, 1024], P('tp', ('dp', 'ctx'))
- out_first_new: float32 [1024, 1024], P('tp', ('dp', 'ctx'))
- out_second_new: float32 [1024, 1024], P('tp', ('dp', 'ctx'))
- out_update: float32 [1024, 1024], P('tp', ('dp', 'ctx'))
- router_grad: float32 [1024, 4], P(('dp', 'ctx'))
- router_first_new: float32 [1024, 4], P(('dp', 'ctx'))
- router_second_new: float32 [1024, 4], P(('dp', 'ctx'))
- router_update: float32 [1024, 4], P(('dp', 'ctx'))
- gains_grad: float32 [2, 1024], P(None, ('dp', 'ctx'))
- gains_first_new: float32 [2, 1024], P(None, ('dp', 'ctx'))
- gains_second_new: float32 [2, 1024], P(None, ('dp', 'ctx'))
- gains_update: float32 [2, 1024], P(None, ('dp', 'ctx'))
- bias_grad: float32 [16, 32], P('tp')
- bias_first_new: float32 [16, 32], P('tp')
- bias_second_new: float32 [16, 32], P('tp')
- bias_update: float32 [16, 32], P('tp')
- in_grad: float32 [4, 2, 1024, 2816], P('dp', None, 'ctx', 'tp')
- in_first_new: float32 [4, 2, 1024, 2816], P('dp', None, 'ctx', 'tp')
- in_second_new: float32 [4, 2, 1024, 2816], P('dp', None, 'ctx', 'tp')
- in_update: float32 [4, 2, 1024, 2816], P('dp', None, 'ctx', 'tp')
- down_grad: float32 [4, 2816, 1024], P('dp', 'tp', 'ctx')
- down_first_new: float32 [4, 2816, 1024], P('dp', 'tp', 'ctx')
- down_second_new: float32 [4, 2816, 1024], P('dp', 'tp', 'ctx')
- down_update: float32 [4, 2816, 1024], P('dp', 'tp', 'ctx')
Inputs may be any that keep to these rules, and one draw needn't show every extreme that they name: `segments`: along each sequence the document number never falls; each document has 1 to 1024 positions, one exactly 1024. `routes`: A token's 2 experts differ; every expert is named by some token.
All inputs are finite; a program needn't handle non-finite values.
Results may differ from a plain program's by a relative error of at most 0.017.
Values may be sent and summed in bfloat16 or wider, within the bound.
A program may use at most 384 MiB of HBM per device.

v0:
```python
import functools

import jax
import jax.numpy as jnp
from jax import lax
from jax.experimental import pallas as pl
from jax.experimental.pallas import tpu as pltpu
from jax.sharding import PartitionSpec as P

D = 1024
HEAD_DIM = 64
BUCKETS = 32

NORM_EPS = 1e-06
NEG_FILL = -1e30
BETA_ONE = 0.9
BETA_TWO = 0.95
FIX_ONE = 1.0 - 0.9**10
FIX_TWO = 1.0 - 0.95**10
ADAM_EPS = 1e-08
WEIGHT_DECAY = 0.1
MAIN_RATE = 0.02
BIAS_RATE = 0.2

F32 = jnp.float32
BF16 = jnp.bfloat16
LANES = 128
BLOCK = 256
VMEM_CAP = 60 * 1024 * 1024
GELU_K = 0.7978845608028654
GELU_C = 0.044715


def tree_sum(values):
    while len(values) > 1:
        values = [values[k] + values[k + 1] for k in range(0, len(values), 2)]
    return values[0]


def rms_scale(values):
    return lax.rsqrt(jnp.mean(values * values, axis=-1, keepdims=True) + NORM_EPS)


def norm_back(values, scale_here, gain_here, gradient):
    weighted = gain_here * gradient
    row_inner = jnp.mean(values * weighted, axis=-1, keepdims=True)
    input_part = scale_here * weighted - values * scale_here**3 * row_inner
    return (input_part, jnp.sum(gradient * values * scale_here, axis=0))


def adamw_step(weight, gradient, first_moment, second_moment, step_rate):
    first_new = BETA_ONE * first_moment + (1.0 - BETA_ONE) * gradient
    second_new = BETA_TWO * second_moment + (1.0 - BETA_TWO) * gradient * gradient
    update = -step_rate * (
        first_new / FIX_ONE / (jnp.sqrt(second_new / FIX_TWO) + ADAM_EPS) + WEIGHT_DECAY * weight
    )
    return (first_new, second_new, update)


def cost(micros):
    return pl.CostEstimate(flops=int(micros * 1.15e9), bytes_accessed=1 << 20, transcendentals=0)


def swap(values, axis, bits):
    count = lax.axis_size(axis)
    return lax.ppermute(values, axis, [(i, i ^ bits) for i in range(count)])


def gather_xor(values, axis):
    pieces = {0: values}
    bit = lax.axis_size(axis) >> 1
    while bit:
        for key in list(pieces):
            pieces[key | bit] = swap(pieces[key], axis, bit)
        bit >>= 1
    return [pieces[m] for m in range(len(pieces))]


def scatter_sum(parts, axis):
    live = dict(enumerate(parts))
    bit = 1
    while bit < lax.axis_size(axis):
        left = {}
        for key in live:
            if key & bit == 0:
                moved = swap(live[key | bit].astype(BF16), axis, bit)
                left[key] = live[key].astype(F32) + moved.astype(F32)
        live = left
        bit <<= 1
    return live[0]


def all_sum(values, axis):
    bit = 1
    while bit < lax.axis_size(axis):
        values = values + swap(values, axis, bit)
        bit <<= 1
    return values


def in_order(pieces, place, dim):
    bit = 1
    while bit < len(pieces):
        odd = (place & bit) > 0
        pieces = [jnp.where(odd, pieces[m ^ bit], pieces[m]) for m in range(len(pieces))]
        bit <<= 1
    return jnp.concatenate(pieces, axis=dim)


MESH = pl.DeviceIdType.MESH


class Wire:
    def __init__(self, sends, receives):
        self.sends, self.receives, self.count, self.copies = sends, receives, 0, []

    def send(self, source, target, **device):
        copy = pltpu.make_async_remote_copy(
            src_ref=source,
            dst_ref=target,
            send_sem=self.sends.at[self.count],
            recv_sem=self.receives.at[self.count],
            device_id=device,
            device_id_type=MESH,
        )
        copy.start()
        self.count += 1
        self.copies.append(Arrival(copy))
        return self.copies[-1]

    def finish(self):
        for copy in self.copies:
            copy.sent()


class Arrival:
    def __init__(self, copy):
        self.copy, self.waited, self.gone = copy, False, False

    def sent(self):
        if not self.gone:
            self.copy.wait_send()
        self.gone = True

    def wait(self):
        if not self.waited:
            self.copy.wait_recv()
        self.waited = True


def greet(partners):
    barrier = pltpu.get_barrier_semaphore()
    for device in partners:
        pl.semaphore_signal(barrier, inc=1, device_id=device, device_id_type=MESH)
    pl.semaphore_wait(barrier, len(partners))


def bits_down(count):
    bits, bit = [], count >> 1
    while bit:
        bits.append(bit)
        bit >>= 1
    return bits


def xor_order(count):
    order = [0]
    for bit in bits_down(count):
        order = order + [k | bit for k in order]
    return order


NT = (((1,), (1,)), ((), ()))
NN = (((1,), (0,)), ((), ()))
TN = (((0,), (0,)), ((), ()))


def mm(left, right, dims=NN):
    return lax.dot_general(left, right, dims, preferred_element_type=F32)


def fold_max(values):
    return jnp.max(values.reshape(values.shape[0] // 8, 8, values.shape[1]), axis=0)


def fold_sum(values):
    return jnp.sum(values.reshape(values.shape[0] // 8, 8, values.shape[1]), axis=0)


def skewed(row):
    width = row.shape[1]
    tall = jnp.broadcast_to(row, (LANES, width))
    return pltpu.roll(tall, width - (LANES - 1), 1, stride=1, stride_axis=0)


def unskew_sum(field):
    half = field.shape[0] // 2
    while half >= 1:
        field = pltpu.roll(field[:half], half, 1) + field[half:]
        half //= 2
    return field


def head_masks(rows):
    lane = lax.broadcasted_iota(jnp.int32, (rows, LANES), 1)
    return [(lane < HEAD_DIM).astype(BF16), (lane >= HEAD_DIM).astype(BF16)]


def score_tile(key_block, query_head, skew_ref, head, first, same):
    scores = mm(key_block, query_head, NT)
    tiles = []
    for s in range(BLOCK // LANES):
        column = pl.multiple_of(first - s * LANES, LANES)
        tiles.append(skew_ref[head, :, pl.ds(column, BLOCK)])
    return jnp.where(same, scores + jnp.concatenate(tiles, axis=0), NEG_FILL)


def bucket_lanes(table_ref):
    row = lax.broadcasted_iota(jnp.int32, (BUCKETS, table_ref.shape[1]), 0)
    return (row == table_ref[0:1, :]).astype(F32)


def spread_bias(bias_ref, table_ref, skew_ref, first=0):
    rows = bias_ref[pl.ds((pl.program_id(0) + first) * 2, 2), :]
    window = jnp.dot(
        jnp.concatenate([rows] * 4, axis=0), bucket_lanes(table_ref),
        precision=lax.Precision.HIGHEST, preferred_element_type=F32,
    )
    for h in range(2):
        skew_ref[h] = skewed(window[h : h + 1, :])


def over_blocks(info_ref, qb, query_blocks, step):
    @pl.loop(0, info_ref[query_blocks + qb, 0])
    def _(i):
        blocks = [info_ref[qb, 2 * i + k] for k in range(2)]
        step(
            [pl.ds(pl.multiple_of(kb * BLOCK, BLOCK), BLOCK) for kb in blocks],
            [info_ref[2 * query_blocks, kb] + qb * BLOCK for kb in blocks],
        )


def attention_kernel(
    first, info_ref, query_ref, key_ref, value_ref, bias_ref, table_ref, doc_row_ref,
    doc_col_ref, *refs,
):
    out_ref, total_ref, skew_ref, flip_ref, score_ref, most_ref, sum_ref, mix_ref = refs[-8:]
    tokens, length = query_ref.shape[0], key_ref.shape[0]
    key_blocks, query_blocks = length // BLOCK, tokens // BLOCK
    masks = head_masks(BLOCK)
    spread_bias(bias_ref, table_ref, skew_ref, first)

    @pl.loop(0, key_blocks)
    def _(kb):
        rows = pl.ds(pl.multiple_of(kb * BLOCK, BLOCK), BLOCK)
        flip_ref[:, rows] = value_ref[rows, :].T

    for qb in range(query_blocks):
        here = slice(qb * BLOCK, (qb + 1) * BLOCK)
        pair = query_ref[here, :] * jnp.asarray(HEAD_DIM**-0.5, BF16)
        query_heads = [pair * mask for mask in masks]
        doc_row = doc_row_ref[0:1, here]
        most_ref[...] = jnp.full_like(most_ref, NEG_FILL)
        sum_ref[...] = jnp.zeros_like(sum_ref)
        mix_ref[...] = jnp.zeros_like(mix_ref)

        def scores(spans, firsts):
            for rows, first_column in zip(spans, firsts):
                column = doc_col_ref[rows, :]
                same = jnp.concatenate([column] * (BLOCK // LANES), axis=1) == doc_row
                for h in range(2):
                    tile = score_tile(
                        key_ref[rows, :], query_heads[h], skew_ref, h, first_column, same
                    )
                    score_ref[h, rows, :] = tile
                    most_ref[h] = jnp.maximum(most_ref[h], fold_max(tile))

        over_blocks(info_ref, qb, query_blocks, scores)
        most = [jnp.max(most_ref[h], axis=0, keepdims=True) for h in range(2)]

        def mixes(spans, firsts):
            for h in range(2):
                heads = slice(h * HEAD_DIM, (h + 1) * HEAD_DIM)
                total, mix = sum_ref[h], mix_ref[h]
                for rows in spans:
                    weights = jnp.exp(score_ref[h, rows, :] - most[h])
                    total += fold_sum(weights)
                    mix += mm(flip_ref[heads, rows], weights.astype(BF16))
                sum_ref[h] = total
                mix_ref[h] = mix

        over_blocks(info_ref, qb, query_blocks, mixes)
        columns = []
        for h in range(2):
            total = jnp.sum(sum_ref[h], axis=0, keepdims=True)
            columns.append(mix_ref[h] / total)
            total_ref[0, h : h + 1, here] = most[h] + jnp.log(total)
        out_ref[here, :] = jnp.concatenate(columns, axis=0).T.astype(BF16)


def attention_back_kernel(
    info_ref, query_ref, key_ref, value_ref, grad_ref, total_ref, bias_ref, table_ref,
    doc_row_ref, doc_col_ref,
    query_grad_ref, key_grad_ref, value_grad_ref, bias_grad_ref,
    skew_ref, field_ref, flip_ref, weight_ref, change_ref, inner_ref, mix_ref, key_sum, value_sum,
):
    tokens, length = query_ref.shape[0], key_ref.shape[0]
    key_blocks, query_blocks = length // BLOCK, tokens // BLOCK
    masks = head_masks(BLOCK)
    spread_bias(bias_ref, table_ref, skew_ref)
    field_ref[...] = jnp.zeros_like(field_ref)
    key_sum[...] = jnp.zeros_like(key_sum)
    value_sum[...] = jnp.zeros_like(value_sum)

    @pl.loop(0, key_blocks)
    def _(kb):
        rows = pl.ds(pl.multiple_of(kb * BLOCK, BLOCK), BLOCK)
        flip_ref[:, rows] = key_ref[rows, :].T

    for qb in range(query_blocks):
        here = slice(qb * BLOCK, (qb + 1) * BLOCK)
        pair = query_ref[here, :] * jnp.asarray(HEAD_DIM**-0.5, BF16)
        query_heads = [pair * mask for mask in masks]
        grad_pair = grad_ref[here, :]
        grad_heads = [grad_pair * mask for mask in masks]
        doc_row = doc_row_ref[0:1, here]
        inner_ref[...] = jnp.zeros_like(inner_ref)
        mix_ref[...] = jnp.zeros_like(mix_ref)
        totals = [total_ref[0, h : h + 1, here] for h in range(2)]

        def changes(spans, firsts):
            for rows, first_column in zip(spans, firsts):
                column = doc_col_ref[rows, :]
                same = jnp.concatenate([column] * (BLOCK // LANES), axis=1) == doc_row
                for h in range(2):
                    tile = score_tile(
                        key_ref[rows, :], query_heads[h], skew_ref, h, first_column, same
                    )
                    weights = jnp.exp(tile - totals[h])
                    change = mm(value_ref[rows, :], grad_heads[h], NT)
                    weight_ref[h, rows, :] = weights
                    change_ref[h, rows, :] = change
                    inner_ref[h] += fold_sum(weights * change)

        over_blocks(info_ref, qb, query_blocks, changes)
        inner = [jnp.sum(inner_ref[h], axis=0, keepdims=True) for h in range(2)]

        def gradients(spans, firsts):
            mixes = [mix_ref[h] for h in range(2)]
            for rows, first_column in zip(spans, firsts):
                key_part = value_part = None
                for h in range(2):
                    weights = weight_ref[h, rows, :]
                    score_grad = weights * (change_ref[h, rows, :] - inner[h])
                    for s in range(BLOCK // LANES):
                        first = pl.multiple_of(first_column - s * LANES, LANES)
                        field_ref[h, :, pl.ds(first, BLOCK)] += score_grad[
                            s * LANES : (s + 1) * LANES
                        ]
                    low = score_grad.astype(BF16)
                    key_here = mm(low, query_heads[h])
                    value_here = mm(weights.astype(BF16), grad_heads[h])
                    key_part = key_here if h == 0 else key_part + key_here
                    value_part = value_here if h == 0 else value_part + value_here
                    heads = slice(h * HEAD_DIM, (h + 1) * HEAD_DIM)
                    mixes[h] += mm(flip_ref[heads, rows], low)
                key_sum[rows, :] += key_part
                value_sum[rows, :] += value_part
            for h in range(2):
                mix_ref[h] = mixes[h]

        over_blocks(info_ref, qb, query_blocks, gradients)
        both = jnp.concatenate([mix_ref[0], mix_ref[1]], axis=0) * HEAD_DIM**-0.5
        query_grad_ref[here, :] = both.T.astype(BF16)

    key_grad_ref[...] = key_sum[...].astype(BF16)
    value_grad_ref[...] = value_sum[...].astype(BF16)
    offsets = jnp.concatenate([unskew_sum(field_ref[h]) for h in range(2)] * 4, axis=0)
    bias_grad_ref[0] = lax.dot_general(
        offsets, bucket_lanes(table_ref), NT, precision=lax.Precision.HIGHEST,
        preferred_element_type=F32,
    )


def attention_specs(tokens, length, pairs, heads, width, first=0):
    smem = pl.BlockSpec(memory_space=pltpu.SMEM)
    return dict(
        info=smem,
        query=pl.BlockSpec((tokens, LANES), lambda i: (0, i + first)),
        key=pl.BlockSpec((length, LANES), lambda i: (0, i + first)),
        value=pl.BlockSpec((length, LANES), lambda i: (0, i + first + pairs)),
        bias=pl.BlockSpec((heads, BUCKETS), lambda i: (0, 0)),
        table=pl.BlockSpec((8, width), lambda i: (0, 0)),
        total=pl.BlockSpec((1, 8, tokens), lambda i: (i + first, 0, 0)),
        bias_grad=pl.BlockSpec((1, 8, BUCKETS), lambda i: (i, 0, 0)),
        doc_row=pl.BlockSpec((8, tokens), lambda i: (0, 0)),
        doc_col=pl.BlockSpec((length, LANES), lambda i: (0, 0)),
    )


def attention(info, queries, key_values, bias, table, doc_row, doc_col, first, count, held):
    tokens, length = queries.shape[0], key_values.shape[0]
    pairs, width = bias.shape[0] // 2, table.shape[1]
    specs = attention_specs(tokens, length, pairs, bias.shape[0], width, first)
    return pl.pallas_call(
        functools.partial(attention_kernel, first),
        grid=(count,),
        in_specs=[
            specs["info"], specs["query"], specs["key"], specs["value"], specs["bias"],
            specs["table"], specs["doc_row"], specs["doc_col"],
        ]
        + [pl.BlockSpec(memory_space=pl.ANY)] * len(held),
        out_specs=[pl.BlockSpec((tokens, LANES), lambda i: (0, i)), specs["total"]],
        out_shape=[
            jax.ShapeDtypeStruct((tokens, count * LANES), BF16),
            jax.ShapeDtypeStruct((pairs, 8, tokens), F32),
        ],
        scratch_shapes=[
            pltpu.VMEM((2, LANES, width), F32),
            pltpu.VMEM((LANES, length), BF16),
            pltpu.VMEM((2, length, BLOCK), F32),
            pltpu.VMEM((2, 8, BLOCK), F32),
            pltpu.VMEM((2, 8, BLOCK), F32),
            pltpu.VMEM((2, HEAD_DIM, BLOCK), F32),
        ],
        input_output_aliases={8: 1} if held else {},
        compiler_params=pltpu.CompilerParams(vmem_limit_bytes=VMEM_CAP),
        cost_estimate=cost(5),
        name="attention_forward",
    )(info, queries, key_values, key_values, bias, table, doc_row, doc_col, *held)


def attention_back(info, queries, key_values, grads, totals, bias, table, doc_row, doc_col):
    tokens, length = queries.shape[0], key_values.shape[0]
    pairs, width = bias.shape[0] // 2, table.shape[1]
    specs = attention_specs(tokens, length, pairs, bias.shape[0], width)
    return pl.pallas_call(
        attention_back_kernel,
        grid=(pairs,),
        in_specs=[
            specs["info"], specs["query"], specs["key"], specs["value"], specs["query"],
            specs["total"], specs["bias"], specs["table"], specs["doc_row"], specs["doc_col"],
        ],
        out_specs=[specs["query"], specs["key"], specs["key"], specs["bias_grad"]],
        out_shape=[
            jax.ShapeDtypeStruct(queries.shape, BF16),
            jax.ShapeDtypeStruct((length, queries.shape[1]), BF16),
            jax.ShapeDtypeStruct((length, queries.shape[1]), BF16),
            jax.ShapeDtypeStruct((pairs, 8, BUCKETS), F32),
        ],
        scratch_shapes=[
            pltpu.VMEM((2, LANES, width), F32),
            pltpu.VMEM((2, LANES, width), F32),
            pltpu.VMEM((LANES, length), BF16),
            pltpu.VMEM((2, length, BLOCK), F32),
            pltpu.VMEM((2, length, BLOCK), F32),
            pltpu.VMEM((2, 8, BLOCK), F32),
            pltpu.VMEM((2, HEAD_DIM, BLOCK), F32),
            pltpu.VMEM((length, LANES), F32),
            pltpu.VMEM((length, LANES), F32),
        ],
        compiler_params=pltpu.CompilerParams(vmem_limit_bytes=VMEM_CAP),
        cost_estimate=cost(40),
        name="attention_backward",
    )(info, queries, key_values, key_values, grads, totals, bias, table, doc_row, doc_col)


def start_kernel(
    experts, dp_count, ctx_count, tp_count, qkv_ref, out_flip_ref, router_ref, gain_pair_ref,
    hidden_ref, segments_ref, routes_ref, out_grad_ref, expert_ref,
    query_ref, pair_ref, normed_flip_ref, weight_out, own_ref, lanes_ref, gains_ref, info_ref,
    row_ref, column_ref, picker_ref, picker_rows_ref, grads_own_ref, grads_ref, early_land,
    expert_land,
    weights, out_all, hidden, docs, docs_ref, flip, sends, receives, out_sem,
):
    d, c, t = lax.axis_index("dp"), lax.axis_index("ctx"), lax.axis_index("tp")
    rows = out_flip_ref.shape[0]
    tokens, width = query_ref.shape
    early = early_blocks(dp_count)
    own_rows = pl.ds(pl.multiple_of((d * ctx_count + c) * rows, rows), rows)
    own_lanes = pl.ds(pl.multiple_of(t * width, width), width)
    for part in range(3):
        weights[own_rows, part * width : (part + 1) * width] = qkv_ref[part]
    out_all[own_rows, own_lanes] = out_flip_ref[...]
    flip[...] = jnp.zeros_like(flip)
    flip[:experts, :rows] = router_ref[...].astype(F32)
    flip[experts : experts + 2, :rows] = gain_pair_ref[...].astype(F32)
    weights[own_rows, 3 * width :] = flip[:, :LANES].T[:rows].astype(BF16)
    docs_ref[...] = jnp.broadcast_to(segments_ref[...], docs_ref.shape)
    row_ref[...] = docs_ref[...]
    greet(
        [{"ctx": c ^ m} for m in range(1, ctx_count)]
        + [{"dp": d ^ m} for m in sorted(set(bits_down(dp_count) + early))]
        + [{"tp": t ^ k} for k in range(1, tp_count)]
    )
    wire = Wire(sends, receives)
    share = grads_ref.shape[2]
    own_share = pl.ds(pl.multiple_of(t * share, share), share)

    def send_shard(m, j, part, lanes=own_lanes, **device):
        index = (d ^ m) * ctx_count + (c ^ j)
        here = pl.ds(pl.multiple_of(index * rows, rows), rows)
        shard = out_all.at[here, lanes] if part else weights.at[here]
        return wire.send(shard, shard, **device)

    docs_sent = [wire.send(docs_ref, docs.at[m], ctx=c ^ m) for m in range(1, ctx_count)]
    sides, sides_far = [0], []
    parts = (0, 1)
    arrivals = {part: [] for part in range(2)}
    hidden_sent, expert_sent = {}, {}
    for bit in bits_down(ctx_count)[:-1]:
        arrivals = {
            k: [send_shard(0, j, part, ctx=c ^ bit) for j in sides]
            for k, part in enumerate(parts)
        }
        assert bit == 2
        half = hidden_ref.at[:, own_share]
        hidden_sent[2] = wire.send(half, hidden.at[2, :, own_share], ctx=c ^ 2)
        for m in [0] + list(expert_sent):
            if m:
                expert_sent[m].wait()
            source = expert_land.at[m - 1] if m else expert_ref
            expert_sent[m | bit] = wire.send(source, expert_land.at[(m | bit) - 1], ctx=c ^ bit)
        for copy in arrivals[0]:
            copy.wait()
        sides_far = sides + [j | bit for j in sides]
        if bit != 2:
            for copy in arrivals[1]:
                copy.wait()
        sides = sides_far
    hidden_sent[1] = wire.send(hidden_ref, hidden.at[1], ctx=c ^ 1)

    order = xor_order(dp_count)
    groups = [{}, {}]
    crossed, beside = [[], []], []

    def onward(k, m):
        for copy in groups[k].get(m, []):
            copy.wait()
        for bit in bits_down(dp_count):
            if m & (2 * bit - 1) == 0:
                groups[k][m | bit] = [send_shard(m, j, parts[k], dp=d ^ bit) for j in sides]
        crossed[k] += [send_shard(m, j, parts[k], ctx=c ^ 1) for j in sides]
        if k:
            for other in range(1, tp_count):
                beside.append(
                    (m, other, [send_shard(m, j, 1, tp=t ^ other) for j in sides])
                )

    onward(0, 0)
    for copy in arrivals[1]:
        copy.wait()
    onward(1, 0)
    expert_sent[1] = wire.send(expert_ref, expert_land.at[0], ctx=c ^ 1)

    lane = lax.broadcasted_iota(jnp.int32, (tokens, LANES), 1)
    flip[:8, :] = jnp.zeros((8, tokens), F32)
    flip[: routes_ref.shape[0], :] = routes_ref[...].astype(F32)
    routes = flip[...].T
    tops = [routes[:, k : k + 1].astype(jnp.int32) for k in range(routes_ref.shape[0])]
    named = jnp.zeros((tokens, LANES), F32)
    for top in tops:
        named = jnp.where(lane == top, 1.0, named)
    row_index = lax.broadcasted_iota(jnp.int32, (tokens, tokens), 0)
    column_index = lax.broadcasted_iota(jnp.int32, (tokens, tokens), 1)
    before = jnp.where(column_index < row_index, 1.0, 0.0).astype(BF16)
    earlier = mm(before, named.astype(BF16))
    slots = grads_own_ref.shape[0]
    column = lax.broadcasted_iota(jnp.int32, picker_ref.shape, 1)
    picker = jnp.zeros(picker_ref.shape, F32)
    for top in tops:
        place = jnp.sum(jnp.where(lane == top, earlier, 0.0), axis=1, keepdims=True)
        place = place.astype(jnp.int32)
        target = jnp.where(place < slots, (top ^ d) * slots + place, -1)
        picker = jnp.where(column == target, 1.0, picker)
    picker_ref[...] = picker.astype(BF16)
    picker_rows_ref[...] = picker_ref[...].T
    hidden_sent[2].wait()
    half = hidden.at[2, :, own_share]
    spread = [wire.send(half, half, tp=t ^ k) for k in range(1, tp_count)]
    for m in range(dp_count):
        chosen = picker_rows_ref[m * slots : (m + 1) * slots, :]
        if m:
            grads_ref[m - 1] = mm(chosen, out_grad_ref[:, own_share]).astype(BF16)
        else:
            grads_own_ref[...] = mm(chosen, out_grad_ref[...]).astype(BF16)

    key_blocks, query_blocks = tokens // BLOCK, tokens // BLOCK
    where = lax.broadcasted_iota(jnp.int32, info_ref.shape, 1)
    which = lax.broadcasted_iota(jnp.int32, info_ref.shape, 0)
    info = jnp.zeros(info_ref.shape, jnp.int32)
    met = [[] for _ in range(query_blocks)]
    for m in range(ctx_count):
        if m:
            docs_sent[m - 1].wait()
        row = docs[m] if m else docs_ref[...]
        tall = jnp.broadcast_to(row[0:1, :].astype(F32), (LANES, tokens))
        column_ref[m * tokens : (m + 1) * tokens, :] = tall.T.astype(jnp.int32)
        for k in range(key_blocks):
            spot = m * key_blocks + k
            low = row[0:1, k * BLOCK : k * BLOCK + 1]
            high = row[0:1, (k + 1) * BLOCK - 1 : (k + 1) * BLOCK]
            for q in range(query_blocks):
                query_low = docs_ref[0:1, q * BLOCK : q * BLOCK + 1]
                query_high = docs_ref[0:1, (q + 1) * BLOCK - 1 : (q + 1) * BLOCK]
                meets = ((high >= query_low) & (low <= query_high)).astype(jnp.int32)
                met[q].append(meets)
            base = (ctx_count * tokens - LANES) - ((c ^ m) * tokens + k * BLOCK)
            info = jnp.where((where == spot) & (which == 2 * query_blocks), base, info)
    for q in range(query_blocks):
        count = sum(met[q][1:], met[q][0])
        inside, outside = jnp.zeros_like(count), count
        for spot, meets in enumerate(met[q]):
            place = jnp.where(meets > 0, inside, outside)
            info = jnp.where((where == place) & (which == q), spot, info)
            inside, outside = inside + meets, outside + (1 - meets)
        steps = lax.shift_right_logical(count + 1, 1)
        info = jnp.where(which == query_blocks + q, steps, info)
    info_ref[...] = info

    early_copies = []
    for i, m in enumerate(order[1:]):
        onward(0, m)
        onward(1, m)
        if i == 0:
            early_copies = [
                wire.send(grads_ref.at[n - 1], early_land.at[k], dp=d ^ n)
                for k, n in enumerate(early)
            ]
    for copy in spread:
        copy.wait()
    hidden_sent[3] = wire.send(hidden.at[2], hidden.at[3], ctx=c ^ 1)
    for copy in crossed[0]:
        copy.wait()
    keep = pltpu.make_async_copy(weights.at[:, : 3 * width], weight_out, out_sem.at[0])
    keep.start()
    small = weights[:, 3 * width : 3 * width + LANES].astype(F32)
    lane = lax.broadcasted_iota(jnp.int32, small.shape, 1)
    lanes_ref[...] = jnp.where(lane < experts, small, 0.0).astype(BF16)
    gain_one = jnp.sum(jnp.where(lane == experts, small, 0.0), axis=1, keepdims=True)
    gain_two = jnp.sum(jnp.where(lane == experts + 1, small, 0.0), axis=1, keepdims=True)
    both = jnp.where(lane == 0, gain_one, jnp.where(lane == 1, gain_two, 0.0)).T
    gains_ref[...] = both[:8]
    gain = both[0:1]
    for m in range(ctx_count):
        if m:
            hidden_sent[m].wait()
        values = (hidden[m] if m else hidden_ref[...]).astype(F32)
        scale = lax.rsqrt(jnp.mean(values * values, axis=-1, keepdims=True) + NORM_EPS)
        normed = (values * scale * gain).astype(BF16)
        pair_ref[m * tokens : (m + 1) * tokens, :] = mm(
            normed, weights[:, width : 3 * width]
        ).astype(BF16)
        if m == 0:
            normed_flip_ref[...] = normed.T
            query_ref[...] = mm(normed, weights[:, :width]).astype(BF16)
            for n, other, copies in beside:
                for copy in copies:
                    copy.wait()
                lanes = pl.ds(pl.multiple_of((t ^ other) * width, width), width)
                crossed[1] += [send_shard(n, j, 1, lanes, ctx=c ^ 1) for j in sides]
    for copy in crossed[1]:
        copy.wait()
    keep_own = pltpu.make_async_copy(out_all, own_ref, out_sem.at[1])
    keep_own.start()
    for k in [k for k in expert_sent if k > 1]:
        expert_sent[k].wait()
        expert_sent[k | 1] = wire.send(expert_land.at[k - 1], expert_land.at[k], ctx=c ^ 1)
    for k in range(1, ctx_count):
        expert_sent[k].wait()
    for copy in early_copies:
        copy.wait()
    keep.wait()
    keep_own.wait()
    wire.finish()


def early_blocks(dp_count):
    return list(range(2, dp_count))[:1]


def start(qkv, out_flip, router, gain_pair, hidden, segments, routes, out_grad, expert, slots):
    tokens, (experts, _), width = hidden.shape[0], router.shape, qkv.shape[2]
    columns = 4 * width + LANES
    dp_count, ctx_count, tp_count = (lax.axis_size(a) for a in ("dp", "ctx", "tp"))
    copies = 5 * ctx_count + (2 + tp_count) * dp_count * ctx_count + tp_count + dp_count + 1
    vmem = pl.BlockSpec(memory_space=pltpu.VMEM)
    hbm = pl.BlockSpec(memory_space=pl.ANY)
    shape = jax.ShapeDtypeStruct
    return pl.pallas_call(
        functools.partial(start_kernel, experts, dp_count, ctx_count, tp_count),
        in_specs=[vmem] * 8 + [hbm],
        out_specs=[vmem] * 3 + [hbm] * 2 + [vmem] * 9 + [hbm] * 2,
        out_shape=[
            shape((tokens, width), BF16),
            shape((tokens * ctx_count, 2 * width), BF16),
            shape((D, tokens), BF16),
            shape((D, 3 * width), BF16),
            shape((D, tp_count * width), BF16),
            shape((D, LANES), BF16),
            shape((8, D), F32),
            shape((8, LANES), jnp.int32),
            shape((8, tokens), jnp.int32),
            shape((tokens * ctx_count, LANES), jnp.int32),
            shape((tokens, dp_count * slots), BF16),
            shape((dp_count * slots, tokens), BF16),
            shape((slots, D), BF16),
            shape((dp_count - 1, slots, D // tp_count), BF16),
            shape((len(early_blocks(dp_count)), slots, D // tp_count), BF16),
            shape((ctx_count - 1,) + expert.shape, BF16),
        ],
        scratch_shapes=[
            pltpu.VMEM((D, columns - width), BF16),
            pltpu.VMEM((D, tp_count * width), BF16),
            pltpu.VMEM((ctx_count, tokens, D), BF16),
            pltpu.VMEM((ctx_count, 8, tokens), jnp.int32),
            pltpu.VMEM((8, tokens), jnp.int32),
            pltpu.VMEM((LANES, tokens), F32),
            pltpu.SemaphoreType.DMA((copies,)),
            pltpu.SemaphoreType.DMA((copies,)),
            pltpu.SemaphoreType.DMA((2,)),
        ],
        compiler_params=pltpu.CompilerParams(
            vmem_limit_bytes=VMEM_CAP, collective_id=1, has_side_effects=True
        ),
        cost_estimate=cost(60),
        name="start",
    )(qkv, out_flip, router, gain_pair, hidden, segments, routes, out_grad, expert)


def bent_parts(value):
    square = value * value
    wave = jnp.tanh(GELU_K * value * (1.0 + GELU_C * square))
    half = 0.5 * (1.0 + wave)
    slope = half + 0.5 * value * (1.0 - wave * wave) * (GELU_K * (1.0 + 3.0 * GELU_C * square))
    return value * half, slope


def expert_kernel(
    experts, dp_count, ctx_count, tp_count, attended_ref, hidden_ref, out_grad_ref, gains_ref,
    lanes_ref, picker_ref, picker_rows_ref, *refs,
):
    d, c, t = lax.axis_index("dp"), lax.axis_index("ctx"), lax.axis_index("tp")
    firsts, refs = refs[:tp_count], refs[tp_count:]
    out_ref, grads_own, refs = refs[0], refs[1], refs[2:]
    grads_land, refs = refs[: dp_count - 1], refs[dp_count - 1 :]
    in_own, in_land, refs = refs[0], refs[1], refs[2:]
    ins = [in_own] + [in_land.at[j] for j in range(ctx_count - 1)]
    down_own, refs = refs[0], refs[1:]
    middle_ref, router_grad_ref, grad_ref, low_ref, attended_grad_ref, gain_ref = refs[:6]
    out_parts, refs = refs[6 : 6 + tp_count], refs[6 + tp_count :]
    (attended_out, in_keep, in_core, in_sum, down_keep, down_core, down_far,
     mixed, out_all, in_all, down_all, rows_all, scaled_all, act_all, gate_all, up_all, send_rows,
     row_parts, row_in, row_back, dot_parts, dot_in, dot_home, dot_back, probs, whole,
     normed_flip, in_land_far, down_land_far,
     sends, receives, in_sems, keep_sems) = refs
    tokens, second_width = attended_ref.shape
    first_width = firsts[0].shape[1]
    width = first_width + second_width
    share = D // tp_count
    slots = rows_all.shape[0] // dp_count
    depth, ff = in_own.shape[1], in_own.shape[2]
    shares = range(1, tp_count)
    order = [0] + list(range(2, dp_count)) + [1]

    local = []

    def load(source, target):
        copy = pltpu.make_async_copy(source, target, in_sems.at[len(local)])
        copy.start()
        local.append(copy)
        return copy

    out_copies = [load(out_ref, out_all)]
    weight_copies, down_parts = [], []
    for j in range(ctx_count):
        part = slice(j * depth, (j + 1) * depth)
        weight_copies.append(load(ins[j], in_all.at[:, part, :]))
        down_parts.append(down_all.at[:, part])
    weight_copies.append(load(down_own, down_parts[0]))
    own_share = pl.ds(pl.multiple_of(t * share, share), share)
    weight_copies.append(load(grads_own, scaled_all.at[:slots]))
    grad_copies = [
        load(grads_land[m - 1], scaled_all.at[m * slots : (m + 1) * slots, own_share])
        for m in range(1, dp_count)
    ]
    own_lanes = pl.ds(pl.multiple_of(t * width, width), width)
    second_lanes = pl.ds(pl.multiple_of(t * width + first_width, LANES), second_width)
    mixed[:, second_lanes] = attended_ref[...]
    for m in range(tp_count):
        start = pl.multiple_of((t ^ m) * width, width)
        mixed[:, pl.ds(start, first_width)] = firsts[m][...]
    attended_out[...] = mixed[:, own_lanes]
    greet(
        [{"tp": t ^ k} for k in shares]
        + [{"dp": d ^ m} for m in range(1, dp_count)]
        + [{"ctx": c ^ 1}, {"ctx": c ^ 2}]
    )
    wire = Wire(sends, receives)
    assert ctx_count == 4
    downs = {j: wire.send(down_own, down_parts[j], ctx=c ^ j) for j in (2, 1)}
    second_part = mixed.at[:, second_lanes]
    arrivals = [wire.send(second_part, second_part, tp=t ^ k) for k in shares]
    spread, returned, dot_returned = {}, {}, {}
    for copy in grad_copies:
        copy.wait()

    def spread_grads(m):
        half = scaled_all.at[m * slots : (m + 1) * slots, own_share]
        spread[m] = [wire.send(half, half, tp=t ^ k) for k in shares]

    for m in order[1:]:
        spread_grads(m)
    for copy in out_copies:
        copy.wait()
    for copy in arrivals:
        copy.wait()
    middle = hidden_ref[...].astype(F32) + mm(mixed[...], out_all[...], NT)
    middle_ref[...] = middle
    scale = lax.rsqrt(jnp.mean(middle * middle, axis=-1, keepdims=True) + NORM_EPS)
    normed = (middle * scale * gains_ref[1:2, :]).astype(BF16)
    far = {}

    def block(m):
        return slice(m * slots, (m + 1) * slots)

    for m in order[1:] + [0]:
        picked = mm(picker_rows_ref[block(m), :], normed).astype(BF16)
        if m:
            send_rows[m - 1] = picked
            far[m] = wire.send(
                send_rows.at[m - 1, :, own_share], rows_all.at[block(m), own_share], dp=d ^ m
            )
        else:
            rows_all[block(0), :] = picked
    lane = lax.broadcasted_iota(jnp.int32, (tokens, LANES), 1)

    def router_probs(values):
        logits = mm(values, lanes_ref[...])
        where = lax.broadcasted_iota(jnp.int32, logits.shape, 1)
        logits = jnp.where(where < experts, logits, NEG_FILL)
        powers = jnp.exp(logits - jnp.max(logits, axis=1, keepdims=True))
        return where, powers / jnp.sum(powers, axis=1, keepdims=True)

    probs[...] = router_probs(normed)[1]
    normed_flip[...] = normed.T
    for copy in weight_copies:
        copy.wait()
    downs[2].wait()
    downs[3] = wire.send(down_parts[2], down_parts[3], ctx=c ^ 1)
    downs[1].wait()
    downs[3].wait()
    columns = [pl.ds(pl.multiple_of((c ^ j) * depth, depth), depth) for j in range(ctx_count)]

    def forward(m):
        far[m].wait()
        half = rows_all.at[block(m), own_share]
        spread[m] += [wire.send(half, half, tp=t ^ k) for k in shares]

    def experts_on(m, hook):
        here = block(m)
        where, chance = router_probs(rows_all[here, :])
        gate = jnp.sum(jnp.where(where == d, chance, 0.0), axis=1, keepdims=True)
        rows = jnp.concatenate([rows_all[here, part] for part in columns], axis=1)
        grad_rows = jnp.concatenate([scaled_all[here, part] for part in columns], axis=1)
        rows_all[here, :] = rows
        scaled_all[here, :] = (gate * grad_rows.astype(F32)).astype(BF16)
        dots = jnp.zeros((slots, LANES), F32)
        for first in range(0, ff, BLOCK):
            part = slice(first, min(ff, first + BLOCK))
            value = mm(rows, in_all[0, :, part])
            up = mm(rows, in_all[1, :, part])
            back = mm(grad_rows, down_all[part, :], NT)
            bent, slope = bent_parts(value)
            act = (bent * up).astype(BF16)
            act_all[here, part] = act
            dots += jnp.sum(act.astype(F32) * back, axis=1, keepdims=True)
            scaled = gate * back
            gate_all[here, part] = (scaled * up * slope).astype(BF16)
            up_all[here, part] = (scaled * bent).astype(BF16)
        if hook is not None:
            hook()
        dot_parts[m] = dots.T[:8]
        dot_returned[m] = [
            wire.send(dot_parts.at[m], dot_in.at[k - 1, m], tp=t ^ k) for k in shares
        ]
        for k in list(shares) + [0]:
            for i in range(share // depth):
                piece = ((t ^ k) * (share // depth) + i) ^ c
                part = pl.ds(pl.multiple_of(piece * depth, depth), depth)
                row = mm(gate_all[here, :], in_all[0, part, :], NT)
                row += mm(up_all[here, :], in_all[1, part, :], NT)
                row_parts[k, m, :, i * depth : (i + 1) * depth] = row.astype(BF16)
            if k:
                returned.setdefault(m, []).append(
                    wire.send(row_parts.at[k, m], row_in.at[k - 1, m], tp=t ^ k)
                )
        for k in range(tp_count):
            for i in range(share // depth):
                piece = ((t ^ k) * (share // depth) + i) ^ c
                part = pl.ds(pl.multiple_of(piece * depth, depth), depth)
                out_parts[k][m, :, i * depth : (i + 1) * depth] = (
                    gate * mm(act_all[here, :], down_all[:, part])
                ).astype(BF16)

    homeward = []

    def send_home(m):
        for copy in dot_returned[m]:
            copy.wait()
        dots = tree_sum([dot_parts[m]] + [dot_in[k - 1, m] for k in shares])
        total = row_parts[0, m].astype(F32)
        for k, copy in zip(shares, returned[m]):
            copy.wait()
            total = total + row_in[k - 1, m].astype(F32)
        if m:
            dot_home[m] = dots
            row_parts[0, m] = total.astype(BF16)
            homeward.append(wire.send(dot_home.at[m], dot_back.at[m], dp=d ^ m))
            homeward.append(wire.send(row_parts.at[0, m], row_back.at[block(m)], dp=d ^ m))
        else:
            dot_back[0] = dots
            row_back[block(0), :] = total.astype(BF16)

    for i, m in enumerate(order):
        for copy in spread.get(m, []):
            copy.wait()
            copy.sent()
        hook = functools.partial(forward, order[i + 1]) if i + 1 < len(order) else None
        experts_on(m, hook)
        if i:
            send_home(order[i - 1])

    def in_grads(j):
        part = slice(j * depth, (j + 1) * depth)
        for side, right in enumerate((gate_all, up_all)):
            in_all[side, part, :] = mm(rows_all[:, part], right[...], TN).astype(BF16)

    keeps = []

    def keep(source, target):
        copy = pltpu.make_async_copy(source, target, keep_sems.at[len(keeps)])
        copy.start()
        keeps.append(copy)

    def part_of(j):
        return slice(j * depth, (j + 1) * depth)

    downs[3].sent()
    for first in range(0, ff, BLOCK):
        part = slice(first, min(ff, first + BLOCK))
        down_all[part, :] = mm(act_all[:, part], scaled_all[...], TN).astype(BF16)
    near = [
        wire.send(down_parts[3], down_land_far, ctx=c ^ 1),
        wire.send(down_parts[1], down_core, ctx=c ^ 1),
    ]
    keep(down_parts[0], down_keep)
    send_home(order[-1])
    in_grads(3)
    near.append(wire.send(in_all.at[:, part_of(3), :], in_land_far, ctx=c ^ 1))
    near[0].wait()
    down_all[:, part_of(2)] = (
        down_all[:, part_of(2)].astype(F32) + down_land_far[...].astype(F32)
    ).astype(BF16)
    near.append(wire.send(down_parts[2], down_far, ctx=c ^ 2))
    in_grads(1)
    near.append(wire.send(in_all.at[:, part_of(1), :], in_core, ctx=c ^ 1))
    in_grads(2)
    near[2].wait()
    for side in range(2):
        in_all[side, part_of(2), :] = (
            in_all[side, part_of(2), :].astype(F32) + in_land_far[side].astype(F32)
        ).astype(BF16)
    keep(in_all.at[:, part_of(2), :], in_sum)
    in_grads(0)
    keep(in_all.at[:, part_of(0), :], in_keep)

    for copy in homeward:
        copy.wait()
    result = mm(picker_ref[...], row_back[...])
    prob_grad = jnp.zeros((tokens, LANES), F32)
    for m in range(dp_count):
        high = dot_back[m].astype(BF16)
        rest = dot_back[m] - high.astype(F32)
        middle_part = rest.astype(BF16)
        tiny = (rest - middle_part.astype(F32)).astype(BF16)
        total = mm(picker_ref[:, block(m)], high, NT)
        total += mm(picker_ref[:, block(m)], middle_part, NT)
        total += mm(picker_ref[:, block(m)], tiny, NT)
        prob_grad = jnp.where(lane == (d ^ m), total[:, 0:1], prob_grad)
    chance = probs[...]
    logit = chance * (prob_grad - jnp.sum(chance * prob_grad, axis=1, keepdims=True))
    more = lax.dot_general(
        logit, lanes_ref[own_share, :].astype(F32), NT, precision=lax.Precision.HIGHEST,
        preferred_element_type=F32,
    )
    whole[:, own_share] = (result + more).astype(BF16)
    arrivals = [wire.send(whole.at[:, own_share], whole.at[:, own_share], tp=t ^ k) for k in shares]
    logit_high = logit.astype(BF16)
    logit_rest = logit - logit_high.astype(F32)
    logit_low = logit_rest.astype(BF16)
    logit_tiny = (logit_rest - logit_low.astype(F32)).astype(BF16)
    router_grad = mm(normed_flip[...], logit_high)
    router_grad += mm(normed_flip[...], logit_low)
    router_grad += mm(normed_flip[...], logit_tiny)
    router_grad_ref[...] = router_grad
    for copy in arrivals:
        copy.wait()
    middle = middle_ref[...]
    gradient = whole[...].astype(F32)
    scale = lax.rsqrt(jnp.mean(middle * middle, axis=-1, keepdims=True) + NORM_EPS)
    weighted = gains_ref[1:2, :] * gradient
    inner = jnp.mean(middle * weighted, axis=-1, keepdims=True)
    gain_ref[...] = fold_sum(gradient * middle * scale)
    total = out_grad_ref[...].astype(F32) + (
        scale * weighted - middle * (scale * scale * scale) * inner
    )
    grad_ref[...] = total
    low_ref[...] = total.astype(BF16)
    attended_grad_ref[...] = mm(low_ref[...], out_all[:, own_lanes]).astype(BF16)
    for copy in keeps:
        copy.wait()
    for copy in near:
        copy.wait()
    wire.finish()


def expert_step(
    firsts, attended, hidden, out_grad, gains, lanes, picker_flip, picker_rows, out, grads_own,
    grads, expert, expert_land, down, experts,
):
    dp_count, ctx_count, tp_count = (lax.axis_size(a) for a in ("dp", "ctx", "tp"))
    tokens, width = attended.shape[0], firsts[0].shape[1] + attended.shape[1]
    slots = grads_own.shape[0]
    share = D // tp_count
    depth, ff = expert.shape[1], expert.shape[2]
    all_slots = dp_count * slots
    others = tp_count - 1
    copies = others * (2 + 4 * dp_count) + 3 * dp_count + 8
    vmem = pl.BlockSpec(memory_space=pltpu.VMEM)
    hbm = pl.BlockSpec(memory_space=pl.ANY)
    shape = jax.ShapeDtypeStruct
    return pl.pallas_call(
        functools.partial(expert_kernel, experts, dp_count, ctx_count, tp_count),
        in_specs=[vmem] * (7 + tp_count) + [hbm] * (4 + dp_count),
        out_specs=[vmem] * (7 + tp_count) + [hbm] * 6,
        out_shape=[
            shape((tokens, D), F32),
            shape((D, LANES), F32),
            shape((tokens, D), F32),
            shape((tokens, D), BF16),
            shape((tokens, width), BF16),
            shape((8, D), F32),
        ]
        + [shape((dp_count, slots, share), BF16)] * tp_count
        + [shape((tokens, width), BF16)]
        + [shape((2, depth, ff), BF16)] * 3
        + [shape((ff, depth), BF16)] * 3,
        scratch_shapes=[
            pltpu.VMEM((tokens, tp_count * width), BF16),
            pltpu.VMEM((D, tp_count * width), BF16),
            pltpu.VMEM((2, D, ff), BF16),
            pltpu.VMEM((ff, D), BF16),
            pltpu.VMEM((all_slots, D), BF16),
            pltpu.VMEM((all_slots, D), BF16),
            pltpu.VMEM((all_slots, ff), BF16),
            pltpu.VMEM((all_slots, ff), BF16),
            pltpu.VMEM((all_slots, ff), BF16),
            pltpu.VMEM((dp_count - 1, slots, D), BF16),
            pltpu.VMEM((tp_count, dp_count, slots, share), BF16),
            pltpu.VMEM((others, dp_count, slots, share), BF16),
            pltpu.VMEM((all_slots, share), BF16),
            pltpu.VMEM((dp_count, 8, slots), F32),
            pltpu.VMEM((others, dp_count, 8, slots), F32),
            pltpu.VMEM((dp_count, 8, slots), F32),
            pltpu.VMEM((dp_count, 8, slots), F32),
            pltpu.VMEM((tokens, LANES), F32),
            pltpu.VMEM((tokens, D), BF16),
            pltpu.VMEM((D, tokens), BF16),
            pltpu.VMEM((2, depth, ff), BF16),
            pltpu.VMEM((ff, depth), BF16),
            pltpu.SemaphoreType.DMA((copies,)),
            pltpu.SemaphoreType.DMA((copies,)),
            pltpu.SemaphoreType.DMA((2 + ctx_count + dp_count,)),
            pltpu.SemaphoreType.DMA((3,)),
        ],
        compiler_params=pltpu.CompilerParams(
            vmem_limit_bytes=VMEM_CAP, collective_id=3, has_side_effects=True
        ),
        cost_estimate=cost(120),
        name="expert_step",
    )(
        attended, hidden, out_grad, gains, lanes, picker_flip, picker_rows, *firsts, out,
        grads_own, *grads, expert, expert_land, down,
    )


def final_kernel(
    experts, dp_count, ctx_count, tp_count,
    query_grad_ref, key_ref, value_ref, normed_ref, weight_ref, low_ref, attended_ref,
    router_grad_ref, hidden_ref, gains_ref, gain_two_ref, middle_grad_ref, middle_ref,
    picker_ref, bias_ref, *refs,
):
    outs, refs = refs[:tp_count], refs[tp_count:]
    (input_grad_ref, output_ref, bias_out_ref, first_ref, second_ref, tail_ref, out_sum, out_back,
     mixed, bias_send, bias_in,
    key_in, send_far, far_in, first_all, second_all, first_core, second_core, first_sum,
    second_sum, first_dp, second_dp, first_x, second_x, rows_all, token_grad, token_in,
    gain_send, gain_in, sends, receives) = refs
    d, c, t = lax.axis_index("dp"), lax.axis_index("ctx"), lax.axis_index("tp")
    tokens, width = query_grad_ref.shape
    dp_bits = bits_down(dp_count)[::-1]
    far_bits = bits_down(ctx_count)[:-1][::-1]
    far = list(range(0, ctx_count, 2))
    greet(
        [{"ctx": c ^ bit} for bit in bits_down(ctx_count)]
        + [{"dp": d ^ m} for m in range(1, dp_count)]
        + [{"tp": t ^ k} for k in range(1, tp_count)]
    )
    wire = Wire(sends, receives)

    bias_steps = [{"ctx": c ^ bit} for bit in bits_down(ctx_count)[::-1]]
    bias_steps += [{"dp": d ^ bit} for bit in dp_bits]
    bias_total, bias_copies = [bias_ref[...]], []

    def bias_begin():
        level = len(bias_copies)
        bias_send[level] = bias_total[-1]
        bias_copies.append(
            wire.send(bias_send.at[level], bias_in.at[level], **bias_steps[level])
        )

    def bias_end():
        level = len(bias_copies) - 1
        bias_copies[level].wait()
        bias_total.append(bias_total[-1] + bias_in[level])

    bias_begin()

    slots, share = out_sum.shape[1], out_sum.shape[2]
    own_share = pl.ds(pl.multiple_of(t * share, share), share)
    out_home = []
    for m in list(range(2, dp_count)) + [1, 0]:
        total = tree_sum([out[m].astype(F32) for out in outs]).astype(BF16)
        if m:
            out_sum[m - 1] = total
            out_home.append(
                wire.send(
                    out_sum.at[m - 1], out_back.at[m * slots : (m + 1) * slots], dp=d ^ m
                )
            )
        else:
            out_back[:slots, :] = total

    near = []
    for k in far[::-1]:
        rows = slice((k + 1) * tokens, (k + 2) * tokens)
        for side, ref in enumerate((key_ref, value_ref)):
            near.append(wire.send(ref.at[rows], key_in.at[side, k // 2], ctx=c ^ 1))

    def split(values):
        return values.astype(BF16).reshape(dp_count, ctx_count, -1, values.shape[1])

    def cross(whole, landed):
        return [wire.send(whole.at[:, c ^ (k + 1)], landed.at[k // 2], ctx=c ^ 1) for k in far]

    def add_core(whole, landed, total, copies):
        for k, copy in zip(far, copies):
            copy.wait()
            own = whole[:, pl.ds(c ^ k, 1)][:, 0]
            total[k // 2] = (own.astype(F32) + landed[k // 2].astype(F32)).astype(BF16)

    def dp_send(total, landed, level, sides):
        copies, bit = [], dp_bits[level]
        for m in range(bit, dp_count, 2 * bit):
            for k in sides:
                spot = landed.at[level, k, d ^ m]
                copies.append((m ^ bit, k, wire.send(total.at[k, d ^ m], spot, dp=d ^ bit)))
        return copies

    def dp_add(total, landed, level, copies):
        for m, k, copy in copies:
            copy.wait()
            own = total[k, pl.ds(d ^ m, 1)][0]
            other = landed[level, k, pl.ds(d ^ m, 1)][0]
            total[k, pl.ds(d ^ m, 1)] = (own.astype(F32) + other.astype(F32)).astype(BF16)[None]

    for copy in near:
        copy.wait()
    for k in far[::-1]:
        rows = slice(k * tokens, (k + 1) * tokens)
        for side, ref in enumerate((key_ref, value_ref)):
            send_far[side, k // 2] = (
                ref[rows, :].astype(F32) + key_in[side, k // 2].astype(F32)
            ).astype(BF16)
    assert len(far_bits) == 1
    far_copies = [
        wire.send(send_far.at[side, 1], far_in.at[side], ctx=c ^ 2) for side in range(2)
    ]

    first_all[:, :, :, :width] = split(mm(normed_ref[...], query_grad_ref[...]))
    first_all[:, :, :, width:] = split(mm(low_ref[...], attended_ref[...], TN))
    first_crossed = cross(first_all, first_core)
    bias_end()
    bias_begin()
    token_grad[...] = mm(query_grad_ref[...], weight_ref[:, :width], NT)
    add_core(first_all, first_core, first_sum, first_crossed)
    bias_end()
    bias_begin()
    first_moving = dp_send(first_sum, first_dp, 0, range(len(far)))
    rows_all[:, :width] = query_grad_ref[...]

    for side in range(2):
        far_copies[side].wait()
        rows_all[:, (side + 1) * width : (side + 2) * width] = (
            send_far[side, 0].astype(F32) + far_in[side].astype(F32)
        ).astype(BF16)
    part = token_grad[...] + mm(rows_all[:, width:], weight_ref[:, width:], NT)
    part_low = part.astype(BF16)
    inputs = hidden_ref[...].astype(F32)
    scale = lax.rsqrt(jnp.mean(inputs * inputs, axis=-1, keepdims=True) + NORM_EPS)
    gain_send[0] = fold_sum(part_low.astype(F32) * inputs * scale)
    token_in[0] = part_low
    gain_total = gain_send[0]
    gain_copies, token_copies = [], []
    tp_bits = bits_down(tp_count)[::-1]
    gain_copies.append(wire.send(gain_send.at[0], gain_in.at[0], tp=t ^ tp_bits[0]))
    token_copies.append(wire.send(token_in.at[0], token_in.at[1], tp=t ^ tp_bits[0]))
    second_all[:, :, :, : 2 * width] = split(mm(normed_ref[...], rows_all[:, width:]))
    for level, bit in enumerate(tp_bits):
        if level:
            gain_send[level] = gain_total
            gain_copies.append(wire.send(gain_send.at[level], gain_in.at[level], tp=t ^ bit))
        gain_copies[level].wait()
        gain_total = gain_total + gain_in[level]
    gain_one = jnp.sum(gain_total, axis=0, keepdims=True)
    gain_two = jnp.sum(gain_two_ref[...], axis=0, keepdims=True)
    row = lax.broadcasted_iota(jnp.int32, (LANES, D), 0)
    gain_rows = jnp.where(row == experts, gain_one, jnp.where(row == experts + 1, gain_two, 0.0))
    second_all[:, :, :, 2 * width :] = split(router_grad_ref[...] + gain_rows.T)
    second_crossed = cross(second_all, second_core)

    add_core(second_all, second_core, second_sum, second_crossed)
    second_far = wire.send(second_sum.at[1], second_x, ctx=c ^ 2)
    for copy in out_home:
        copy.wait()
    mixed[:, own_share] = mm(picker_ref[...], out_back[...]).astype(BF16)
    mixed_part = mixed.at[:, own_share]
    mixed_copies = [wire.send(mixed_part, mixed_part, tp=t ^ k) for k in range(1, tp_count)]
    first_far, second_moving = None, None
    for level in range(len(dp_bits)):
        dp_add(first_sum, first_dp, level, first_moving)
        bias_end()
        if level + 1 < len(dp_bits):
            bias_begin()
            first_moving = dp_send(first_sum, first_dp, level + 1, range(len(far)))
        else:
            first_far = wire.send(first_sum.at[1, d], first_x, ctx=c ^ 2)
        if level == 0:
            second_far.wait()
            second_sum[0] = (second_sum[0].astype(F32) + second_x[...].astype(F32)).astype(BF16)
        else:
            dp_add(second_sum, second_dp, level - 1, second_moving)
        second_moving = dp_send(second_sum, second_dp, level, [0])
    total = part_low.astype(F32)
    for level, bit in enumerate(tp_bits):
        if level:
            token_in[2 * level] = total.astype(BF16)
            total = token_in[2 * level].astype(F32)
            token_copies.append(
                wire.send(token_in.at[2 * level], token_in.at[2 * level + 1], tp=t ^ bit)
            )
        token_copies[level].wait()
        total = total + token_in[2 * level + 1].astype(F32)
    weighted = gains_ref[0:1, :] * total
    inner = jnp.mean(inputs * weighted, axis=-1, keepdims=True)
    input_grad_ref[...] = (
        middle_grad_ref[...] + scale * weighted - inputs * (scale * scale * scale) * inner
    )
    for copy in mixed_copies:
        copy.wait()
    output_ref[...] = middle_ref[...] + mixed[...].astype(F32)
    bias_out_ref[...] = bias_total[-1]
    first_far.wait()
    first_ref[...] = first_sum[0, pl.ds(d, 1)][0].astype(F32) + first_x[...].astype(F32)
    dp_add(second_sum, second_dp, len(dp_bits) - 1, second_moving)
    result = second_sum[0, pl.ds(d, 1)][0].astype(F32)
    second_ref[...] = result[:, : 2 * width]
    rest = jnp.zeros((LANES - result.shape[0], LANES), F32)
    tail_ref[...] = jnp.concatenate([result[:, 2 * width :], rest], axis=0).T
    wire.finish()


def final_step(
    query_grad, key_part, value_part, normed, weight, low, attended, router_grad, hidden,
    gains, gain_two, middle_grad, middle, picker, bias, outs, experts,
):
    tokens, width = query_grad.shape
    slots, share = outs[0].shape[1:]
    dp_count, ctx_count, tp_count = (lax.axis_size(a) for a in ("dp", "ctx", "tp"))
    rows = D // (dp_count * ctx_count)
    half = ctx_count // 2
    levels = len(bits_down(dp_count))
    tp_levels = len(bits_down(tp_count))
    one, two = 2 * width, 2 * width + LANES
    copies = 6 * half + 8 + 3 * tp_count + (half + 2) * dp_count + 2 * ctx_count
    vmem = pl.BlockSpec(memory_space=pltpu.VMEM)
    return pl.pallas_call(
        functools.partial(final_kernel, experts, dp_count, ctx_count, tp_count),
        in_specs=[vmem] * (15 + tp_count),
        out_specs=[vmem] * 6,
        out_shape=[
            jax.ShapeDtypeStruct((tokens, D), F32),
            jax.ShapeDtypeStruct((tokens, D), F32),
            jax.ShapeDtypeStruct(bias.shape, F32),
            jax.ShapeDtypeStruct((rows, one), F32),
            jax.ShapeDtypeStruct((rows, 2 * width), F32),
            jax.ShapeDtypeStruct((LANES, LANES), F32),
        ],
        scratch_shapes=[
            pltpu.VMEM((dp_count - 1, slots, share), BF16),
            pltpu.VMEM((dp_count * slots, share), BF16),
            pltpu.VMEM((tokens, D), BF16),
            pltpu.VMEM((levels + ctx_count.bit_length() - 1,) + bias.shape, F32),
            pltpu.VMEM((levels + ctx_count.bit_length() - 1,) + bias.shape, F32),
            pltpu.VMEM((2, half, tokens, width), BF16),
            pltpu.VMEM((2, half, tokens, width), BF16),
            pltpu.VMEM((2, tokens, width), BF16),
            pltpu.VMEM((dp_count, ctx_count, rows, one), BF16),
            pltpu.VMEM((dp_count, ctx_count, rows, two), BF16),
            pltpu.VMEM((half, dp_count, rows, one), BF16),
            pltpu.VMEM((half, dp_count, rows, two), BF16),
            pltpu.VMEM((half, dp_count, rows, one), BF16),
            pltpu.VMEM((half, dp_count, rows, two), BF16),
            pltpu.VMEM((levels, half, dp_count, rows, one), BF16),
            pltpu.VMEM((levels, 1, dp_count, rows, two), BF16),
            pltpu.VMEM((rows, one), BF16),
            pltpu.VMEM((dp_count, rows, two), BF16),
            pltpu.VMEM((tokens, 3 * width), BF16),
            pltpu.VMEM((tokens, D), F32),
            pltpu.VMEM((2 * tp_levels, tokens, D), BF16),
            pltpu.VMEM((tp_levels, 8, D), F32),
            pltpu.VMEM((tp_levels, 8, D), F32),
            pltpu.SemaphoreType.DMA((copies,)),
            pltpu.SemaphoreType.DMA((copies,)),
        ],
        compiler_params=pltpu.CompilerParams(
            vmem_limit_bytes=VMEM_CAP, collective_id=2, has_side_effects=True
        ),
        cost_estimate=cost(87),
        name="final_step",
    )(
        query_grad, key_part, value_part, normed, weight, low, attended, router_grad,
        hidden, gains, gain_two, middle_grad, middle, picker, bias, *outs,
    )


def adam_kernel(*refs):
    weight, first, second = refs[:3]
    parts, outs = refs[3:-4], refs[-4:]
    gradient = parts[0][...].astype(F32) + parts[1][...].astype(F32) + parts[2][...].astype(F32)
    first_new = BETA_ONE * first[...] + (1.0 - BETA_ONE) * gradient
    second_new = BETA_TWO * second[...] + (1.0 - BETA_TWO) * gradient * gradient
    outs[0][...] = gradient
    outs[1][...] = first_new
    outs[2][...] = second_new
    outs[3][...] = -MAIN_RATE * (
        first_new * (1.0 / FIX_ONE) / (jnp.sqrt(second_new * (1.0 / FIX_TWO)) + ADAM_EPS)
        + WEIGHT_DECAY * weight[...].astype(F32)
    )


def adam(weight, first, second, kept, arrived, far):
    count, rows, columns = weight.shape
    step = max(size for size in range(16, rows + 1, 16) if rows % size == 0 and size * columns <= 1 << 17)
    plain = pl.BlockSpec((1, step, columns), lambda i, j: (i, j, 0))
    shape = jax.ShapeDtypeStruct(weight.shape, F32)
    return pl.pallas_call(
        adam_kernel,
        grid=(count, rows // step),
        in_specs=[plain] * 6,
        out_specs=[plain] * 4,
        out_shape=[shape] * 4,
        compiler_params=pltpu.CompilerParams(vmem_limit_bytes=VMEM_CAP),
        cost_estimate=cost(5),
        name="adam",
    )(weight, first, second, kept, arrived, far)


def small_adam_kernel(experts, pairs, *refs):
    first_ref, second_ref, tail_ref, bias_ref = refs[:4]
    inputs, outs = refs[4:19], refs[19:]

    def step(k, gradient, part, rate):
        weight, first, second = (ref[part].astype(F32) for ref in inputs[3 * k : 3 * k + 3])
        first_new = BETA_ONE * first + (1.0 - BETA_ONE) * gradient
        second_new = BETA_TWO * second + (1.0 - BETA_TWO) * gradient * gradient
        update = -rate * (
            first_new * (1.0 / FIX_ONE) / (jnp.sqrt(second_new * (1.0 / FIX_TWO)) + ADAM_EPS)
            + WEIGHT_DECAY * weight
        )
        for out, values in zip(
            outs[4 * k : 4 * k + 4], (gradient, first_new, second_new, update)
        ):
            out[part] = values

    rows, width = inputs[3].shape
    whole = slice(None)
    step(0, first_ref[:, :width], 0, MAIN_RATE)
    step(0, second_ref[:, :width], 1, MAIN_RATE)
    step(0, second_ref[:, width:], 2, MAIN_RATE)
    step(1, first_ref[:, width:], whole, MAIN_RATE)
    step(2, tail_ref[:experts, :rows], whole, MAIN_RATE)
    step(3, tail_ref[experts : experts + 2, :rows], whole, MAIN_RATE)
    bias = jnp.concatenate([bias_ref[p, :2] for p in range(pairs)], axis=0)
    step(4, bias, whole, BIAS_RATE)


def small_adam(first_total, second_total, tail_total, bias_total, triples, experts):
    flat = [array for triple in triples for array in triple]
    vmem = pl.BlockSpec(memory_space=pltpu.VMEM)
    results = pl.pallas_call(
        functools.partial(small_adam_kernel, experts, bias_total.shape[0]),
        in_specs=[vmem] * (4 + len(flat)),
        out_specs=[vmem] * (4 * len(triples)),
        out_shape=[
            jax.ShapeDtypeStruct(triple[0].shape, F32) for triple in triples for _ in range(4)
        ],
        compiler_params=pltpu.CompilerParams(vmem_limit_bytes=VMEM_CAP),
        cost_estimate=cost(2),
        name="small_adam",
    )(first_total, second_total, tail_total, bias_total, *flat)
    return [results[4 * k : 4 * k + 4] for k in range(len(triples))]


def shards(
    hidden_in,
    out_grad,
    segments,
    routes,
    bucket_table,
    qkv_weight,
    out_weight,
    router,
    norm_gains,
    position_bias,
    expert_in,
    expert_down,
    qkv_first,
    qkv_second,
    out_first,
    out_second,
    router_first,
    router_second,
    gains_first,
    gains_second,
    bias_first,
    bias_second,
    in_first,
    in_second,
    down_first,
    down_second,
):
    tokens = hidden_in.shape[0]
    dp_count, ctx_count, tp_count = (lax.axis_size(a) for a in ("dp", "ctx", "tp"))
    dp_place, ctx_place, tp_place = (lax.axis_index(a) for a in ("dp", "ctx", "tp"))
    length = tokens * ctx_count
    heads_here = position_bias.shape[0]
    width_here = heads_here * HEAD_DIM
    pairs = heads_here // 2
    expert_count = router.shape[1]
    top_count = routes.shape[1]
    own_rows = router.shape[0]

    capacity = max(2, min(tokens, 5 * top_count * tokens // (4 * expert_count)))
    window_width = tokens + length
    table = jnp.pad(bucket_table[::-1], (0, 1), constant_values=BUCKETS)
    table = lax.dynamic_slice(table, (ctx_place * tokens,), (window_width,))
    table = jnp.broadcast_to(table[None], (8, window_width))
    qkv_view = [array.transpose(1, 0, 2) for array in (qkv_weight, qkv_first, qkv_second)]
    out_view = [array.T for array in (out_weight, out_first, out_second)]
    router_view = [array.T for array in (router, router_first, router_second)]
    (queries, key_values, normed_flip, qkv_flat, out_own, lanes, gains, info, doc_row, doc_col,
     picker_flip, picker_rows, grads_own, grads_half, early_land, expert_land) = start(
        qkv_view[0], out_view[0], router_view[0], norm_gains, hidden_in, segments, routes.T,
        out_grad, expert_in[0], capacity,
    )
    early = early_blocks(dp_count)
    arrived = [
        early_land[early.index(m)] if m in early else swap(grads_half[m - 1], "dp", m)
        for m in range(1, dp_count)
    ]
    half = pairs // 2
    attended_first, totals = attention(
        info, queries, key_values, position_bias, table, doc_row, doc_col, 0, half, ()
    )
    first_sides = gather_xor(attended_first, "tp")
    attended_second, totals = attention(
        info, queries, key_values, position_bias, table, doc_row, doc_col, half, pairs - half,
        (totals,),
    )
    results = expert_step(
        first_sides, attended_second, hidden_in, out_grad, gains, lanes, picker_flip, picker_rows,
        out_own, grads_own, arrived, expert_in[0], expert_land, expert_down[0], expert_count,
    )
    middle, router_grad, middle_grad, middle_low, attended_grad, gain_two_grad = results[:6]
    out_parts, results = results[6 : 6 + tp_count], results[6 + tp_count :]
    attended, in_keep, in_core, in_sum, down_keep, down_core, down_far = results

    in_far = swap(in_sum, "ctx", 2)
    out_far = [swap(out_parts[k], "tp", k) for k in range(1, tp_count)]
    query_grad, key_part, value_part, bias_part = attention_back(
        info, queries, key_values, attended_grad, totals, position_bias, table, doc_row, doc_col
    )
    query_grad, in_far, out_far = lax.optimization_barrier((query_grad, in_far, out_far))
    input_grad, output, bias_total, first_total, second_total, tail_total = final_step(
        query_grad, key_part, value_part, normed_flip, qkv_flat, middle_low, attended,
        router_grad, hidden_in, gains, gain_two_grad, middle_grad, middle, picker_flip, bias_part,
        [out_parts[0]] + out_far, expert_count,
    )
    qkv_all, out_new, router_new, gains_new, bias_new = small_adam(
        first_total, second_total, tail_total, bias_total,
        [
            qkv_view,
            out_view,
            router_view,
            (norm_gains, gains_first, gains_second),
            (position_bias, bias_first, bias_second),
        ],
        expert_count,
    )
    in_new = [
        values[None]
        for values in adam(
            expert_in[0], in_first[0], in_second[0], in_keep, in_core, in_far
        )
    ]
    down_new = adam(
        expert_down, down_first, down_second, down_keep[None], down_core[None], down_far[None]
    )
    return (
        output,
        input_grad,
        *[array.transpose(1, 0, 2) for array in qkv_all],
        *[array.T for array in out_new],
        *[array.T for array in router_new],
        *gains_new,
        *bias_new,
        *in_new,
        *down_new,
    )


def solution(mesh):
    token_rows = P(("dp", "ctx"), None)
    qkv = P(("dp", "ctx"), None, "tp")
    out = P("tp", ("dp", "ctx"))
    gains = P(None, ("dp", "ctx"))
    bias = P("tp", None)
    expert_in = P("dp", None, "ctx", "tp")
    expert_down = P("dp", "tp", "ctx")
    placed = (
        token_rows, token_rows, P("dp", "ctx"), token_rows, P(),
        qkv, out, token_rows, gains, bias, expert_in, expert_down,
        qkv, qkv, out, out, token_rows, token_rows, gains, gains, bias, bias,
        expert_in, expert_in, expert_down, expert_down,
    )
    return jax.shard_map(
        shards,
        mesh=mesh,
        in_specs=placed,
        out_specs=(token_rows, token_rows)
        + (qkv,) * 4
        + (out,) * 4
        + (token_rows,) * 4
        + (gains,) * 4
        + (bias,) * 4
        + (expert_in,) * 4
        + (expert_down,) * 4,
        check_vma=False,
    )
```

profile of v0, /device:TPU:0, one launch (start us, length us, event | category | flops | bytes accessed | tf_op | source)
XLA Modules:
  0.0 384.2 jit_solution(18047195472478277899)
XLA Ops:
  0.7 0.8 reverse
  1.5 0.1 slice.10
  1.5 0.1 pad_dynamic-slice_fusion
  1.6 74.9 %start.1 = (bf16[512,512]{1,0:T(8,128)(2,1)}, bf16[2048,1024]{1,0:T(8,128)(2,1)}, bf16[1024,512]{1,0:T(8,128)(2,1)}, bf16[1024,1536]{1,0:T(8,128)(2,1)}, bf16[10...) custom-call(bf16[3,64,512]{2,1,0:T(8,128)(2,1)} %bitcast.48, ...), custom_call_target="tpu_custom_call" | custom-call | flops 69000003584 | bytes 1048576 | tf_op jit(solution)/shard_map/start/pallas_call | solution.py:690
  76.6 0.6 broadcast_in_dim.27.table_ref
  77.2 0.0 copy-start.2
  77.2 11.3 %attention_forward.2 = (bf16[512,256]{1,0:T(8,128)(2,1)}, f32[4,8,512]{2,1,0:T(8,128)}) custom-call(s32[8,128]{1,0:T(8,128)} %get-tuple-element.106.info_ref, bf16[512,512]{1,0:T(8,128)(2,1)} %get-tuple-element.107.query_ref, bf16[2048,1024]{1,0:T(8,128)(2,1)} %get-tuple-element.108.key_ref.value_ref, ...), custom_call_target="tpu_custom_call" | custom-call | flops 5750000128 | bytes 1048576 | tf_op jit(solution)/shard_map/attention_forward/pallas_call | solution.py:405
  88.5 0.5 collective-permute-start
  89.0 0.0 copy-done.2
  89.0 1.5 collective-permute-start.2
  90.5 0.0 collective-permute-start.1
  90.5 11.0 %attention_forward.3 = (bf16[512,256]{1,0:T(8,128)(2,1)}, f32[4,8,512]{2,1,0:T(8,128)}) custom-call(s32[8,128]{1,0:T(8,128)} %get-tuple-element.106.info_ref, bf16[512,512]{1,0:T(8,128)(2,1)} %get-tuple-element.107.query_ref, bf16[2048,1024]{1,0:T(8,128)(2,1)} %get-tuple-element.108.key_ref.value_ref, ...), custom_call_target="tpu_custom_call", output_to_operand_aliasing={{1}: (8, {})} | custom-call | flops 5750000128 | bytes 1048576 | tf_op jit(solution)/shard_map/attention_forward/pallas_call | solution.py:405
  101.5 0.0 collective-permute-done.refs_1_
  101.6 0.0 copy-start.7
  101.6 0.0 collective-permute-done.2.refs_6_
  101.6 0.0 copy-start.5
  101.6 6.3 %collective-permute-done.1.refs_4_ = bf16[320,512]{1,0:T(8,128)(2,1)S(1)} collective-permute-done((bf16[320,512]{1,0:T(8,128)(2,1)S(1)}, bf16[320,512]{1,0:T(8,128)(2,1)S(1)}, u32[]{:S(2)}, u32[]{:S(2)}) %collective-permute-start.1) | collective-permute-done | bytes 327712 | tf_op jit(solution)/shard_map/ppermute | solution.py:66
  107.9 0.0 copy-start.6
  107.9 0.0 copy-done.7
  107.9 0.0 copy-done.5
  107.9 0.7 copy-done.6
  108.6 129.5 %expert_step.1 = (f32[512,1024]{1,0:T(8,128)}, f32[1024,128]{1,0:T(8,128)}, f32[512,1024]{1,0:T(8,128)}, bf16[512,1024]{1,0:T(8,128)(2,1)}, bf16[512,512]{1,0:T(...) custom-call(bf16[512,256]{1,0:T(8,128)(2,1)} %get-tuple-element.112., ...), custom_call_target="tpu_custom_call" | custom-call | flops 138000007168 | bytes 1048576 | tf_op jit(solution)/shard_map/expert_step/pallas_call | solution.py:1043
  238.2 1.4 collective-permute-start.4
  239.6 1.1 collective-permute-start.3
  240.7 32.9 %attention_backward.1 = (bf16[512,512]{1,0:T(8,128)(2,1)}, bf16[2048,512]{1,0:T(8,128)(2,1)}, bf16[2048,512]{1,0:T(8,128)(2,1)}, f32[4,8,32]{2,1,0:T(8,128)}) custom-call(s32[8,128]{1,0:T(8,128)} %get-tuple-element.106.info_ref, bf16[512,512]{1,0:T(8,128)(2,1)} %get-tuple-element.107.query_ref, bf16[2048,1024]{1,0:T(8,128)(2,1)} %get-tuple-element.108.key_ref.value_ref, ...), custom_call_target="tpu_custom_call" | custom-call | flops 46000001024 | bytes 1048576 | tf_op jit(solution)/shard_map/attention_backward/pallas_call | solution.py:437
  273.5 5.9 %adam.3 = (f32[1,1408,256]{2,1,0:T(8,128)}, f32[1,1408,256]{2,1,0:T(8,128)}, f32[1,1408,256]{2,1,0:T(8,128)}, f32[1,1408,256]{2,1,0:T(8,128)}) custom-call(bf16[1,1408,256]{2,1,0:T(8,128)(2,1)} %refs_0_.1, f32[1,1408,256]{2,1,0:T(8,128)} %refs_1_.1, f32[1,1408,256]{2,1,0:T(8,128)} %refs_2_.1, bf16[1,1408,256]{2,1,0:T(8,128)(2,1)} %bitcast.63, ...), custom_call_target="tpu_custom_call" | custom-call | flops 5750000128 | bytes 1048576 | tf_op jit(solution)/shard_map/adam/pallas_call | solution.py:1378
  279.4 0.0 collective-permute-done.4.refs_1_
  279.4 0.0 copy-start.4
  279.4 0.0 collective-permute-done.3.refs_5_
  279.4 0.0 copy-start.3
  279.5 1.0 copy-done.4
  280.5 86.2 %final_step.1 = (f32[512,1024]{1,0:T(8,128)}, f32[512,1024]{1,0:T(8,128)}, f32[4,8,32]{2,1,0:T(8,128)}, f32[64,1024]{1,0:T(8,128)}, f32[64,1024]{1,0:T(8,128)}, /*index=5*/f32[128,128]{1,0:T(8,128)}) custom-call(bf16[512,512]{1,0:T(8,128)(2,1)} %get-tuple-element.128.query_grad_ref, bf16[2048,512]{1,0:T(8,128)(2,1)} %get-tuple-element.129.key_ref, ...), custom_call_target="tpu_custom_call" | custom-call | flops 100050001920 | bytes 1048576 | tf_op jit(solution)/shard_map/final_step/pallas_call | solution.py:1308
  366.7 0.0 copy-done.3
  366.7 10.4 %adam.2 = (f32[2,256,1408]{2,1,0:T(8,128)}, f32[2,256,1408]{2,1,0:T(8,128)}, f32[2,256,1408]{2,1,0:T(8,128)}, f32[2,256,1408]{2,1,0:T(8,128)}) custom-call(bf16[2,256,1408]{2,1,0:T(8,128)(2,1)} %bitcast.44, f32[2,256,1408]{2,1,0:T(8,128)} %bitcast.40, f32[2,256,1408]{2,1,0:T(8,128)} %bitcast.41, bf16[2,256,1408]{2,1,0:T(8,128)(2,1)} %get-tuple-element.168.refs_3_, ...), custom_call_target="tpu_custom_call" | custom-call | flops 5750000128 | bytes 1048576 | tf_op jit(solution)/shard_map/adam/pallas_call | solution.py:1378
  377.0 0.0 copy-start.1
  377.0 3.3 small_adam.1
  380.3 0.0 copy-done.1
  380.3 0.0 copy-start
  380.3 1.3 copy.60
  381.7 1.0 copy-done
  382.7 1.3 copy.61
  (1 shorter events, 0.0 us)
Async XLA Ops:
  77.2 11.8 %copy-start.2 = (bf16[3,320,512]{2,1,0:T(8,128)(2,1)S(1)}, bf16[3,320,512]{2,1,0:T(8,128)(2,1)}, u32[]{:S(2)}) copy-start(bf16[3,320,512]{2,1,0:T(8,128)(2,1)} %get-tuple-element.120) | copy-start | bytes 2949124
  88.5 13.1 %collective-permute-start = (bf16[512,256]{1,0:T(8,128)(2,1)}, bf16[512,256]{1,0:T(8,128)(2,1)S(1)}, u32[]{:S(2)}, u32[]{:S(2)}) collective-permute-start(bf16[512,256]{1,0:T(8,128)(2,1)} %get-tuple-element.117.refs_0_), channel_id=1, source_target_pairs={{0,1},{1,0},{2,3},{3,2},{4,5},{5,4},{6,7},{7,6},{8,9},{9,8},{10,11... | collective-permute-start | bytes 786440 | tf_op jit(solution)/shard_map/ppermute | solution.py:66
  89.0 12.5 %collective-permute-start.2 = (bf16[320,512]{1,0:T(8,128)(2,1)S(1)}, bf16[320,512]{1,0:T(8,128)(2,1)S(1)}, u32[]{:S(2)}, u32[]{:S(2)}) collective-permute-start(bf16[320,512]{1,0:T(8,128)(2,1)S(1)} %get-tuple-element.182), channel_id=1, source_target_pairs={{0,24},{8,16},{16,8},{24,0},{1,25},{9,17},{17,9},{25,1},{2,26},{10... | collective-permute-start | bytes 983048 | tf_op jit(solution)/shard_map/ppermute | solution.py:66
  90.5 17.4 %collective-permute-start.1 = (bf16[320,512]{1,0:T(8,128)(2,1)S(1)}, bf16[320,512]{1,0:T(8,128)(2,1)S(1)}, u32[]{:S(2)}, u32[]{:S(2)}) collective-permute-start(bf16[320,512]{1,0:T(8,128)(2,1)S(1)} %get-tuple-element.183), channel_id=1, source_target_pairs={{0,8},{8,0},{16,24},{24,16},{1,9},{9,1},{17,25},{25,17},{2,10},{10... | collective-permute-start | bytes 983048 | tf_op jit(solution)/shard_map/ppermute | solution.py:66
  101.6 6.4 %copy-start.7 = (bf16[512,256]{1,0:T(8,128)(2,1)}, bf16[512,256]{1,0:T(8,128)(2,1)S(1)}, u32[]{:S(2)}) copy-start(bf16[512,256]{1,0:T(8,128)(2,1)S(1)} %collective-permute-done.refs_1_) | copy-start | bytes 786436
  101.6 6.3 %copy-start.5 = (bf16[320,512]{1,0:T(8,128)(2,1)}, bf16[320,512]{1,0:T(8,128)(2,1)S(1)}, u32[]{:S(2)}) copy-start(bf16[320,512]{1,0:T(8,128)(2,1)S(1)} %collective-permute-done.2.refs_6_) | copy-start | bytes 983044
  107.9 0.7 copy-start.6
  238.2 41.2 %collective-permute-start.4 = (bf16[4,320,512]{2,1,0:T(8,128)(2,1)}, bf16[4,320,512]{2,1,0:T(8,128)(2,1)S(1)}, u32[]{:S(2)}, u32[]{:S(2)}) collective-permute-start(bf16[4,320,512]{2,1,0:T(8,128)(2,1)} %get-tuple-element.127), channel_id=1, source_target_pairs={{0,1},{1,0},{2,3},{3,2},{4,5},{5,4},{6,7},{7,6},{8,9},{9,8},{10,11... | collective-permute-start | bytes 3932168 | tf_op jit(solution)/shard_map/ppermute | solution.py:66
  239.6 39.8 %collective-permute-start.3 = (bf16[2,256,1408]{2,1,0:T(8,128)(2,1)}, bf16[2,256,1408]{2,1,0:T(8,128)(2,1)S(1)}, u32[]{:S(2)}, u32[]{:S(2)}) collective-permute-start(bf16[2,256,1408]{2,1,0:T(8,128)(2,1)} %get-tuple-element.126), channel_id=1, source_target_pairs={{0,4},{2,6},{4,0},{6,2},{1,5},{3,7},{5,1},{7,3},{8,12},{10,14},{12... | collective-permute-start | bytes 4325384 | tf_op jit(solution)/shard_map/ppermute | solution.py:66
  279.4 1.1 copy-start.4
  279.4 87.2 %copy-start.3 = (bf16[2,256,1408]{2,1,0:T(8,128)(2,1)}, bf16[2,256,1408]{2,1,0:T(8,128)(2,1)S(1)}, u32[]{:S(2)}) copy-start(bf16[2,256,1408]{2,1,0:T(8,128)(2,1)S(1)} %collective-permute-done.3.refs_5_) | copy-start | bytes 4325380
  377.0 3.3 copy-start.1
  380.3 2.3 copy-start
where the time goes:
time: 389 us; the launch traced here: 384 us
  Pallas kernels  365 us (94%)
  local copies, waits for them, and re-layouts  7.06 us (2%)
  waiting for transfers between devices  6.32 us (2%)
  starting transfers between devices  4.53 us (1%)
    pallas_call x1, Pallas kernels, expert_step(): pl.pallas_call(functools.partial(expert_kernel, experts, dp_count, ctx_co...  130 us
    pallas_call x1, Pallas kernels, final_step(): pl.pallas_call(functools.partial(final_kernel, experts, dp_count, ctx_cou...  86.2 us
    pallas_call x1, Pallas kernels, start(): pl.pallas_call(functools.partial(start_kernel, experts, dp_count, ctx_cou...  74.9 us
    pallas_call x1, Pallas kernels, attention_back(): pl.pallas_call(attention_back_kernel, grid=(pairs,), in_specs=[specs['inf...  32.9 us
    pallas_call x2, Pallas kernels, attention(): pl.pallas_call(functools.partial(attention_kernel, first), grid=(count,),...  22.3 us
    pallas_call x2, Pallas kernels, adam(): pl.pallas_call(adam_kernel, grid=(count, rows // step), in_specs=[plain]...  16.2 us
  transfers between devices with their start and end apart: 5, of which 1 were waited for; matrix products, arithmetic and copies ran while one was open for 0% of the time, Pallas kernels for 13%

commit v1 on v0

--- a/solution.py
+++ b/solution.py
@@ -548,9 +548,6 @@
                 )
 
     onward(0, 0)
-    for copy in arrivals[1]:
-        copy.wait()
-    onward(1, 0)
     expert_sent[1] = wire.send(expert_ref, expert_land.at[0], ctx=c ^ 1)
 
     lane = lax.broadcasted_iota(jnp.int32, (tokens, LANES), 1)
@@ -621,6 +618,11 @@
     early_copies = []
     for i, m in enumerate(order[1:]):
         onward(0, m)
+        if i == 0:
+            for copy in arrivals[1]:
+                copy.wait()
+            onward(1, 0)
+    for i, m in enumerate(order[1:]):
         onward(1, m)
         if i == 0:
             early_copies = [
@@ -737,8 +739,8 @@
 
 
 def expert_kernel(
-    experts, dp_count, ctx_count, tp_count, attended_ref, hidden_ref, out_grad_ref, gains_ref,
-    lanes_ref, picker_ref, picker_rows_ref, *refs,
+    experts, dp_count, ctx_count, tp_count, attended_ref, gains_ref, lanes_ref, hidden_hbm,
+    out_grad_hbm, picker_hbm, picker_rows_hbm, *refs,
 ):
     d, c, t = lax.axis_index("dp"), lax.axis_index("ctx"), lax.axis_index("tp")
     firsts, refs = refs[:tp_count], refs[tp_count:]
@@ -748,12 +750,13 @@
     ins = [in_own] + [in_land.at[j] for j in range(ctx_count - 1)]
     down_own, refs = refs[0], refs[1:]
     middle_ref, router_grad_ref, grad_ref, low_ref, attended_grad_ref, gain_ref = refs[:6]
-    out_parts, refs = refs[6 : 6 + tp_count], refs[6 + tp_count :]
+    out_sums, refs = refs[6 : 4 + dp_count], refs[4 + dp_count :]
+    near_parts, refs = refs[:tp_count], refs[tp_count:]
     (attended_out, in_keep, in_core, in_sum, down_keep, down_core, down_far,
      mixed, out_all, in_all, down_all, rows_all, scaled_all, act_all, gate_all, up_all, send_rows,
      row_parts, row_in, row_back, dot_parts, dot_in, dot_home, dot_back, probs, whole,
-     normed_flip, in_land_far, down_land_far,
-     sends, receives, in_sems, keep_sems) = refs
+     normed_flip, in_land_far, down_land_far, out_parts, out_in, hidden_ref, out_grad_ref,
+     picker_ref, picker_rows_ref, sends, receives, in_sems, keep_sems) = refs
     tokens, second_width = attended_ref.shape
     first_width = firsts[0].shape[1]
     width = first_width + second_width
@@ -771,13 +774,19 @@
         local.append(copy)
         return copy
 
-    out_copies = [load(out_ref, out_all)]
+    out_copies = [
+        load(out_ref, out_all),
+        load(hidden_hbm, hidden_ref),
+        load(picker_rows_hbm, picker_rows_ref),
+    ]
     weight_copies, down_parts = [], []
     for j in range(ctx_count):
         part = slice(j * depth, (j + 1) * depth)
         weight_copies.append(load(ins[j], in_all.at[:, part, :]))
         down_parts.append(down_all.at[:, part])
     weight_copies.append(load(down_own, down_parts[0]))
+    weight_copies.append(load(picker_hbm, picker_ref))
+    weight_copies.append(load(out_grad_hbm, out_grad_ref))
     own_share = pl.ds(pl.multiple_of(t * share, share), share)
     weight_copies.append(load(grads_own, scaled_all.at[:slots]))
     grad_copies = [
@@ -851,6 +860,8 @@
     downs[1].wait()
     downs[3].wait()
     columns = [pl.ds(pl.multiple_of((c ^ j) * depth, depth), depth) for j in range(ctx_count)]
+
+    gates = {}
 
     def forward(m):
         far[m].wait()
@@ -895,12 +906,16 @@
                 returned.setdefault(m, []).append(
                     wire.send(row_parts.at[k, m], row_in.at[k - 1, m], tp=t ^ k)
                 )
+        gates[m] = gate
+
+    def outputs_of(m):
+        here = block(m)
         for k in range(tp_count):
             for i in range(share // depth):
                 piece = ((t ^ k) * (share // depth) + i) ^ c
                 part = pl.ds(pl.multiple_of(piece * depth, depth), depth)
-                out_parts[k][m, :, i * depth : (i + 1) * depth] = (
-                    gate * mm(act_all[here, :], down_all[:, part])
+                out_parts[k, m, :, i * depth : (i + 1) * depth] = (
+                    gates[m] * mm(act_all[here, :], down_all[:, part])
                 ).astype(BF16)
 
     homeward = []
@@ -946,6 +961,15 @@
     def part_of(j):
         return slice(j * depth, (j + 1) * depth)
 
+    for m in order:
+        outputs_of(m)
+    out_copies = [
+        wire.send(out_parts.at[k, m], out_in.at[k - 1, m], tp=t ^ k)
+        for m in order[1:-1]
+        for k in shares
+    ]
+    for k in range(tp_count):
+        near_parts[k][...] = out_parts[k, :2]
     downs[3].sent()
     for first in range(0, ff, BLOCK):
         part = slice(first, min(ff, first + BLOCK))
@@ -1004,6 +1028,11 @@
     router_grad += mm(normed_flip[...], logit_low)
     router_grad += mm(normed_flip[...], logit_tiny)
     router_grad_ref[...] = router_grad
+    for copy in out_copies:
+        copy.wait()
+    for m in range(2, dp_count):
+        parts = [out_parts[0, m]] + [out_in[k - 1, m] for k in shares]
+        out_sums[m - 2][...] = tree_sum([part.astype(F32) for part in parts]).astype(BF16)
     for copy in arrivals:
         copy.wait()
     middle = middle_ref[...]
@@ -1036,14 +1065,14 @@
     depth, ff = expert.shape[1], expert.shape[2]
     all_slots = dp_count * slots
     others = tp_count - 1
-    copies = others * (2 + 4 * dp_count) + 3 * dp_count + 8
+    copies = others * (2 + 5 * dp_count) + 3 * dp_count + 8
     vmem = pl.BlockSpec(memory_space=pltpu.VMEM)
     hbm = pl.BlockSpec(memory_space=pl.ANY)
     shape = jax.ShapeDtypeStruct
     return pl.pallas_call(
         functools.partial(expert_kernel, experts, dp_count, ctx_count, tp_count),
-        in_specs=[vmem] * (7 + tp_count) + [hbm] * (4 + dp_count),
-        out_specs=[vmem] * (7 + tp_count) + [hbm] * 6,
+        in_specs=[vmem] * 3 + [hbm] * 4 + [vmem] * tp_count + [hbm] * (4 + dp_count),
+        out_specs=[vmem] * (5 + dp_count + tp_count) + [hbm] * 6,
         out_shape=[
             shape((tokens, D), F32),
             shape((D, LANES), F32),
@@ -1052,7 +1081,8 @@
             shape((tokens, width), BF16),
             shape((8, D), F32),
         ]
-        + [shape((dp_count, slots, share), BF16)] * tp_count
+        + [shape((slots, share), BF16)] * (dp_count - 2)
+        + [shape((2, slots, share), BF16)] * tp_count
         + [shape((tokens, width), BF16)]
         + [shape((2, depth, ff), BF16)] * 3
         + [shape((ff, depth), BF16)] * 3,
@@ -1079,9 +1109,15 @@
             pltpu.VMEM((D, tokens), BF16),
             pltpu.VMEM((2, depth, ff), BF16),
             pltpu.VMEM((ff, depth), BF16),
+            pltpu.VMEM((tp_count, dp_count, slots, share), BF16),
+            pltpu.VMEM((others, dp_count, slots, share), BF16),
+            pltpu.VMEM((tokens, D), BF16),
+            pltpu.VMEM((tokens, D), BF16),
+            pltpu.VMEM((tokens, all_slots), BF16),
+            pltpu.VMEM((all_slots, tokens), BF16),
             pltpu.SemaphoreType.DMA((copies,)),
             pltpu.SemaphoreType.DMA((copies,)),
-            pltpu.SemaphoreType.DMA((2 + ctx_count + dp_count,)),
+            pltpu.SemaphoreType.DMA((6 + ctx_count + dp_count,)),
             pltpu.SemaphoreType.DMA((3,)),
         ],
         compiler_params=pltpu.CompilerParams(
@@ -1090,37 +1126,47 @@
         cost_estimate=cost(120),
         name="expert_step",
     )(
-        attended, hidden, out_grad, gains, lanes, picker_flip, picker_rows, *firsts, out,
+        attended, gains, lanes, hidden, out_grad, picker_flip, picker_rows, *firsts, out,
         grads_own, *grads, expert, expert_land, down,
     )
 
 
 def final_kernel(
     experts, dp_count, ctx_count, tp_count,
-    query_grad_ref, key_ref, value_ref, normed_ref, weight_ref, low_ref, attended_ref,
-    router_grad_ref, hidden_ref, gains_ref, gain_two_ref, middle_grad_ref, middle_ref,
-    picker_ref, bias_ref, *refs,
+    key_ref, value_ref, gains_ref, gain_two_ref, bias_ref, *refs,
 ):
-    outs, refs = refs[:tp_count], refs[tp_count:]
-    (input_grad_ref, output_ref, bias_out_ref, first_ref, second_ref, tail_ref, out_sum, out_back,
-     mixed, bias_send, bias_in,
-    key_in, send_far, far_in, first_all, second_all, first_core, second_core, first_sum,
-    second_sum, first_dp, second_dp, first_x, second_x, rows_all, token_grad, token_in,
-    gain_send, gain_in, sends, receives) = refs
+    late, refs = refs[:10], refs[10:]
+    near_outs, refs = refs[:tp_count], refs[tp_count:]
+    far_outs, refs = refs[: dp_count - 2], refs[dp_count - 2 :]
+    (input_grad_ref, output_ref, bias_out_ref, first_ref, second_ref, tail_ref, out_back,
+     mixed, bias_send, bias_in, near_in, far_send, far_in, rows_all, token_grad, token_in,
+     gain_send, gain_in, out_send) = refs[:19]
+    first, value, key = (refs[19 + 5 * k : 24 + 5 * k] for k in range(3))
+    targets, refs = refs[34:44], refs[44:]
+    (query_grad_ref, normed_ref, low_ref, attended_ref, weight_ref, hidden_ref,
+     router_grad_ref, picker_ref, middle_ref, middle_grad_ref) = targets
+    near_land, (sends, receives, late_sems, near_sems) = refs[:tp_count], refs[tp_count:]
+    loads = [
+        pltpu.make_async_copy(source, target, late_sems.at[k])
+        for k, (source, target) in enumerate(zip(late, targets))
+    ]
+    near_loads = [
+        pltpu.make_async_copy(source, target, near_sems.at[k])
+        for k, (source, target) in enumerate(zip(near_outs, near_land))
+    ]
     d, c, t = lax.axis_index("dp"), lax.axis_index("ctx"), lax.axis_index("tp")
     tokens, width = query_grad_ref.shape
     dp_bits = bits_down(dp_count)[::-1]
-    far_bits = bits_down(ctx_count)[:-1][::-1]
-    far = list(range(0, ctx_count, 2))
+    assert ctx_count == 4
+    halves = (0, 1)
     greet(
-        [{"ctx": c ^ bit} for bit in bits_down(ctx_count)]
-        + [{"dp": d ^ m} for m in range(1, dp_count)]
+        [{"ctx": c ^ 1}, {"ctx": c ^ 2}]
+        + [{"dp": d ^ bit} for bit in dp_bits]
         + [{"tp": t ^ k} for k in range(1, tp_count)]
     )
     wire = Wire(sends, receives)
 
-    bias_steps = [{"ctx": c ^ bit} for bit in bits_down(ctx_count)[::-1]]
-    bias_steps += [{"dp": d ^ bit} for bit in dp_bits]
+    bias_steps = [{"ctx": c ^ 1}, {"ctx": c ^ 2}] + [{"dp": d ^ bit} for bit in dp_bits]
     bias_total, bias_copies = [bias_ref[...]], []
 
     def bias_begin():
@@ -1135,90 +1181,120 @@
         bias_copies[level].wait()
         bias_total.append(bias_total[-1] + bias_in[level])
 
-    bias_begin()
-
-    slots, share = out_sum.shape[1], out_sum.shape[2]
-    own_share = pl.ds(pl.multiple_of(t * share, share), share)
-    out_home = []
-    for m in list(range(2, dp_count)) + [1, 0]:
-        total = tree_sum([out[m].astype(F32) for out in outs]).astype(BF16)
-        if m:
-            out_sum[m - 1] = total
-            out_home.append(
-                wire.send(
-                    out_sum.at[m - 1], out_back.at[m * slots : (m + 1) * slots], dp=d ^ m
-                )
-            )
-        else:
-            out_back[:slots, :] = total
-
-    near = []
-    for k in far[::-1]:
-        rows = slice((k + 1) * tokens, (k + 2) * tokens)
-        for side, ref in enumerate((key_ref, value_ref)):
-            near.append(wire.send(ref.at[rows], key_in.at[side, k // 2], ctx=c ^ 1))
-
     def split(values):
         return values.astype(BF16).reshape(dp_count, ctx_count, -1, values.shape[1])
 
-    def cross(whole, landed):
-        return [wire.send(whole.at[:, c ^ (k + 1)], landed.at[k // 2], ctx=c ^ 1) for k in far]
-
-    def add_core(whole, landed, total, copies):
-        for k, copy in zip(far, copies):
+    def cross(part):
+        return [
+            wire.send(part[0].at[:, c ^ (2 * k + 1)], part[1].at[k], ctx=c ^ 1) for k in halves
+        ]
+
+    def add_core(part, copies):
+        for k, copy in zip(halves, copies):
             copy.wait()
-            own = whole[:, pl.ds(c ^ k, 1)][:, 0]
-            total[k // 2] = (own.astype(F32) + landed[k // 2].astype(F32)).astype(BF16)
-
-    def dp_send(total, landed, level, sides):
+            own = part[0][:, pl.ds(c ^ (2 * k), 1)][:, 0]
+            part[2][k] = (own.astype(F32) + part[1][k].astype(F32)).astype(BF16)
+
+    def dp_send(part, level, sides):
         copies, bit = [], dp_bits[level]
         for m in range(bit, dp_count, 2 * bit):
             for k in sides:
-                spot = landed.at[level, k, d ^ m]
-                copies.append((m ^ bit, k, wire.send(total.at[k, d ^ m], spot, dp=d ^ bit)))
+                spot = part[3].at[level, k, d ^ m]
+                copies.append((m ^ bit, k, wire.send(part[2].at[k, d ^ m], spot, dp=d ^ bit)))
         return copies
 
-    def dp_add(total, landed, level, copies):
+    def dp_add(part, level, copies):
         for m, k, copy in copies:
             copy.wait()
-            own = total[k, pl.ds(d ^ m, 1)][0]
-            other = landed[level, k, pl.ds(d ^ m, 1)][0]
-            total[k, pl.ds(d ^ m, 1)] = (own.astype(F32) + other.astype(F32)).astype(BF16)[None]
-
-    for copy in near:
-        copy.wait()
-    for k in far[::-1]:
-        rows = slice(k * tokens, (k + 1) * tokens)
-        for side, ref in enumerate((key_ref, value_ref)):
-            send_far[side, k // 2] = (
-                ref[rows, :].astype(F32) + key_in[side, k // 2].astype(F32)
+            own = part[2][k, pl.ds(d ^ m, 1)][0]
+            other = part[3][level, k, pl.ds(d ^ m, 1)][0]
+            part[2][k, pl.ds(d ^ m, 1)] = (own.astype(F32) + other.astype(F32)).astype(BF16)[None]
+
+    def x_send(part):
+        return wire.send(part[2].at[1], part[4], ctx=c ^ 2)
+
+    def x_add(part, copy):
+        copy.wait()
+        part[2][0] = (part[2][0].astype(F32) + part[4][...].astype(F32)).astype(BF16)
+
+    bias_begin()
+    sources = (value_ref, key_ref)
+    near = [
+        [
+            wire.send(ref.at[(2 * k + 1) * tokens : (2 * k + 2) * tokens], near_in.at[side, k],
+                      ctx=c ^ 1)
+            for k in (1, 0)
+        ]
+        for side, ref in enumerate(sources)
+    ]
+    slots, share = out_send.shape
+    far_loads = [
+        pltpu.make_async_copy(
+            source, out_back.at[(k + 2) * slots : (k + 3) * slots], near_sems.at[tp_count + k]
+        )
+        for k, source in enumerate(far_outs)
+    ]
+    for copy in near_loads + loads + far_loads:
+        copy.start()
+    for copy in near_loads:
+        copy.wait()
+    sums = [tree_sum([land[m].astype(F32) for land in near_land]) for m in range(2)]
+    out_back[:slots, :] = sums[0].astype(BF16)
+    out_send[...] = sums[1].astype(BF16)
+    out_home = wire.send(out_send, out_back.at[slots : 2 * slots], dp=d ^ 1)
+    far_copies = []
+    for side, ref in enumerate(sources):
+        for k, copy in zip((1, 0), near[side]):
+            copy.wait()
+            rows = slice(2 * k * tokens, (2 * k + 1) * tokens)
+            far_send[side, k] = (
+                ref[rows, :].astype(F32) + near_in[side, k].astype(F32)
             ).astype(BF16)
-    assert len(far_bits) == 1
-    far_copies = [
-        wire.send(send_far.at[side, 1], far_in.at[side], ctx=c ^ 2) for side in range(2)
-    ]
-
-    first_all[:, :, :, :width] = split(mm(normed_ref[...], query_grad_ref[...]))
-    first_all[:, :, :, width:] = split(mm(low_ref[...], attended_ref[...], TN))
-    first_crossed = cross(first_all, first_core)
+            if k:
+                if side == 0:
+                    bias_end()
+                    bias_begin()
+                far_copies.append(wire.send(far_send.at[side, 1], far_in.at[side], ctx=c ^ 2))
+
+    for copy in loads[:5]:
+        copy.wait()
+    first[0][:, :, :, :width] = split(mm(normed_ref[...], query_grad_ref[...]))
+    first[0][:, :, :, width:] = split(mm(low_ref[...], attended_ref[...], TN))
+    first_crossed = cross(first)
+    token_grad[...] = mm(query_grad_ref[...], weight_ref[:, :width], NT)
+    add_core(first, first_crossed)
     bias_end()
     bias_begin()
-    token_grad[...] = mm(query_grad_ref[...], weight_ref[:, :width], NT)
-    add_core(first_all, first_core, first_sum, first_crossed)
-    bias_end()
-    bias_begin()
-    first_moving = dp_send(first_sum, first_dp, 0, range(len(far)))
-    rows_all[:, :width] = query_grad_ref[...]
-
-    for side in range(2):
+    first_moving = dp_send(first, 0, halves)
+    for copy in loads[5:]:
+        copy.wait()
+    out_home.wait()
+    for copy in far_loads:
+        copy.wait()
+    own_share = pl.ds(pl.multiple_of(t * share, share), share)
+    mixed[:, own_share] = mm(picker_ref[...], out_back[...]).astype(BF16)
+    mixed_part = mixed.at[:, own_share]
+    mixed_copies = [wire.send(mixed_part, mixed_part, tp=t ^ k) for k in range(1, tp_count)]
+
+    def land(side, columns):
         far_copies[side].wait()
-        rows_all[:, (side + 1) * width : (side + 2) * width] = (
-            send_far[side, 0].astype(F32) + far_in[side].astype(F32)
+        rows_all[:, columns] = (
+            far_send[side, 0].astype(F32) + far_in[side].astype(F32)
         ).astype(BF16)
-    part = token_grad[...] + mm(rows_all[:, width:], weight_ref[:, width:], NT)
-    part_low = part.astype(BF16)
+
+    key_columns, value_columns = slice(width, 2 * width), slice(2 * width, 3 * width)
+    land(0, value_columns)
+    value[0][...] = split(mm(normed_ref[...], rows_all[:, value_columns]))
+    value_crossed = cross(value)
+    token_grad[...] += mm(rows_all[:, value_columns], weight_ref[:, value_columns], NT)
+    add_core(value, value_crossed)
+    value_far = x_send(value)
     inputs = hidden_ref[...].astype(F32)
     scale = lax.rsqrt(jnp.mean(inputs * inputs, axis=-1, keepdims=True) + NORM_EPS)
+
+    land(1, key_columns)
+    part = token_grad[...] + mm(rows_all[:, key_columns], weight_ref[:, key_columns], NT)
+    part_low = part.astype(BF16)
     gain_send[0] = fold_sum(part_low.astype(F32) * inputs * scale)
     token_in[0] = part_low
     gain_total = gain_send[0]
@@ -1226,7 +1302,7 @@
     tp_bits = bits_down(tp_count)[::-1]
     gain_copies.append(wire.send(gain_send.at[0], gain_in.at[0], tp=t ^ tp_bits[0]))
     token_copies.append(wire.send(token_in.at[0], token_in.at[1], tp=t ^ tp_bits[0]))
-    second_all[:, :, :, : 2 * width] = split(mm(normed_ref[...], rows_all[:, width:]))
+    key[0][:, :, :, :width] = split(mm(normed_ref[...], rows_all[:, key_columns]))
     for level, bit in enumerate(tp_bits):
         if level:
             gain_send[level] = gain_total
@@ -1237,31 +1313,27 @@
     gain_two = jnp.sum(gain_two_ref[...], axis=0, keepdims=True)
     row = lax.broadcasted_iota(jnp.int32, (LANES, D), 0)
     gain_rows = jnp.where(row == experts, gain_one, jnp.where(row == experts + 1, gain_two, 0.0))
-    second_all[:, :, :, 2 * width :] = split(router_grad_ref[...] + gain_rows.T)
-    second_crossed = cross(second_all, second_core)
-
-    add_core(second_all, second_core, second_sum, second_crossed)
-    second_far = wire.send(second_sum.at[1], second_x, ctx=c ^ 2)
-    for copy in out_home:
-        copy.wait()
-    mixed[:, own_share] = mm(picker_ref[...], out_back[...]).astype(BF16)
-    mixed_part = mixed.at[:, own_share]
-    mixed_copies = [wire.send(mixed_part, mixed_part, tp=t ^ k) for k in range(1, tp_count)]
-    first_far, second_moving = None, None
+    key[0][:, :, :, width:] = split(router_grad_ref[...] + gain_rows.T)
+    key_crossed = cross(key)
+    add_core(key, key_crossed)
+    key_far = x_send(key)
+
+    moving = {}
+    first_far = None
     for level in range(len(dp_bits)):
-        dp_add(first_sum, first_dp, level, first_moving)
+        dp_add(first, level, first_moving)
         bias_end()
         if level + 1 < len(dp_bits):
             bias_begin()
-            first_moving = dp_send(first_sum, first_dp, level + 1, range(len(far)))
+            first_moving = dp_send(first, level + 1, halves)
         else:
-            first_far = wire.send(first_sum.at[1, d], first_x, ctx=c ^ 2)
-        if level == 0:
-            second_far.wait()
-            second_sum[0] = (second_sum[0].astype(F32) + second_x[...].astype(F32)).astype(BF16)
-        else:
-            dp_add(second_sum, second_dp, level - 1, second_moving)
-        second_moving = dp_send(second_sum, second_dp, level, [0])
+            first_far = wire.send(first[2].at[1, d], first[4], ctx=c ^ 2)
+        for name, weights, copy in (("value", value, value_far), ("key", key, key_far)):
+            if level == 0:
+                x_add(weights, copy)
+            else:
+                dp_add(weights, level - 1, moving[name])
+            moving[name] = dp_send(weights, level, [0])
     total = part_low.astype(F32)
     for level, bit in enumerate(tp_bits):
         if level:
@@ -1277,17 +1349,20 @@
     input_grad_ref[...] = (
         middle_grad_ref[...] + scale * weighted - inputs * (scale * scale * scale) * inner
     )
-    for copy in mixed_copies:
-        copy.wait()
-    output_ref[...] = middle_ref[...] + mixed[...].astype(F32)
     bias_out_ref[...] = bias_total[-1]
     first_far.wait()
-    first_ref[...] = first_sum[0, pl.ds(d, 1)][0].astype(F32) + first_x[...].astype(F32)
-    dp_add(second_sum, second_dp, len(dp_bits) - 1, second_moving)
-    result = second_sum[0, pl.ds(d, 1)][0].astype(F32)
-    second_ref[...] = result[:, : 2 * width]
+    first_ref[...] = first[2][0, pl.ds(d, 1)][0].astype(F32) + first[4][...].astype(F32)
+    last = len(dp_bits) - 1
+    dp_add(value, last, moving["value"])
+    second_ref[:, width:] = value[2][0, pl.ds(d, 1)][0].astype(F32)
+    dp_add(key, last, moving["key"])
+    result = key[2][0, pl.ds(d, 1)][0].astype(F32)
+    second_ref[:, :width] = result[:, :width]
     rest = jnp.zeros((LANES - result.shape[0], LANES), F32)
-    tail_ref[...] = jnp.concatenate([result[:, 2 * width :], rest], axis=0).T
+    tail_ref[...] = jnp.concatenate([result[:, width:], rest], axis=0).T
+    for copy in mixed_copies:
+        copy.wait()
+    output_ref[...] = middle_ref[...] + mixed[...].astype(F32)
     wire.finish()
 
 
@@ -1299,60 +1374,71 @@
     slots, share = outs[0].shape[1:]
     dp_count, ctx_count, tp_count = (lax.axis_size(a) for a in ("dp", "ctx", "tp"))
     rows = D // (dp_count * ctx_count)
-    half = ctx_count // 2
     levels = len(bits_down(dp_count))
     tp_levels = len(bits_down(tp_count))
-    one, two = 2 * width, 2 * width + LANES
-    copies = 6 * half + 8 + 3 * tp_count + (half + 2) * dp_count + 2 * ctx_count
+    copies = 7 + 2 + levels + 3 * 2 + 4 * dp_count + 3 + 2 * tp_levels + tp_count
+    hbm = pl.BlockSpec(memory_space=pl.ANY)
     vmem = pl.BlockSpec(memory_space=pltpu.VMEM)
+    shape = jax.ShapeDtypeStruct
+
+    late = (
+        query_grad, normed, low, attended, weight, hidden, router_grad, picker, middle,
+        middle_grad,
+    )
+
+    def buffers(columns, far_shape, sides):
+        return [
+            pltpu.VMEM((dp_count, ctx_count, rows, columns), BF16),
+            pltpu.VMEM((2, dp_count, rows, columns), BF16),
+            pltpu.VMEM((2, dp_count, rows, columns), BF16),
+            pltpu.VMEM((levels, sides, dp_count, rows, columns), BF16),
+            pltpu.VMEM(far_shape + (columns,), BF16),
+        ]
+
     return pl.pallas_call(
         functools.partial(final_kernel, experts, dp_count, ctx_count, tp_count),
-        in_specs=[vmem] * (15 + tp_count),
+        in_specs=[vmem] * 5 + [hbm] * (10 + len(outs)),
         out_specs=[vmem] * 6,
         out_shape=[
-            jax.ShapeDtypeStruct((tokens, D), F32),
-            jax.ShapeDtypeStruct((tokens, D), F32),
-            jax.ShapeDtypeStruct(bias.shape, F32),
-            jax.ShapeDtypeStruct((rows, one), F32),
-            jax.ShapeDtypeStruct((rows, 2 * width), F32),
-            jax.ShapeDtypeStruct((LANES, LANES), F32),
+            shape((tokens, D), F32),
+            shape((tokens, D), F32),
+            shape(bias.shape, F32),
+            shape((rows, 2 * width), F32),
+            shape((rows, 2 * width), F32),
+            shape((LANES, LANES), F32),
         ],
         scratch_shapes=[
-            pltpu.VMEM((dp_count - 1, slots, share), BF16),
             pltpu.VMEM((dp_count * slots, share), BF16),
             pltpu.VMEM((tokens, D), BF16),
-            pltpu.VMEM((levels + ctx_count.bit_length() - 1,) + bias.shape, F32),
-            pltpu.VMEM((levels + ctx_count.bit_length() - 1,) + bias.shape, F32),
-            pltpu.VMEM((2, half, tokens, width), BF16),
-            pltpu.VMEM((2, half, tokens, width), BF16),
+            pltpu.VMEM((2 + levels,) + bias.shape, F32),
+            pltpu.VMEM((2 + levels,) + bias.shape, F32),
+            pltpu.VMEM((2, 2, tokens, width), BF16),
+            pltpu.VMEM((2, 2, tokens, width), BF16),
             pltpu.VMEM((2, tokens, width), BF16),
-            pltpu.VMEM((dp_count, ctx_count, rows, one), BF16),
-            pltpu.VMEM((dp_count, ctx_count, rows, two), BF16),
-            pltpu.VMEM((half, dp_count, rows, one), BF16),
-            pltpu.VMEM((half, dp_count, rows, two), BF16),
-            pltpu.VMEM((half, dp_count, rows, one), BF16),
-            pltpu.VMEM((half, dp_count, rows, two), BF16),
-            pltpu.VMEM((levels, half, dp_count, rows, one), BF16),
-            pltpu.VMEM((levels, 1, dp_count, rows, two), BF16),
-            pltpu.VMEM((rows, one), BF16),
-            pltpu.VMEM((dp_count, rows, two), BF16),
             pltpu.VMEM((tokens, 3 * width), BF16),
             pltpu.VMEM((tokens, D), F32),
             pltpu.VMEM((2 * tp_levels, tokens, D), BF16),
             pltpu.VMEM((tp_levels, 8, D), F32),
             pltpu.VMEM((tp_levels, 8, D), F32),
+            pltpu.VMEM((slots, share), BF16),
+        ]
+        + buffers(2 * width, (rows,), 2)
+        + buffers(width, (dp_count, rows), 1)
+        + buffers(width + LANES, (dp_count, rows), 1)
+        + [pltpu.VMEM(array.shape, array.dtype) for array in late]
+        + [pltpu.VMEM((2, slots, share), BF16)] * tp_count
+        + [
             pltpu.SemaphoreType.DMA((copies,)),
             pltpu.SemaphoreType.DMA((copies,)),
+            pltpu.SemaphoreType.DMA((10,)),
+            pltpu.SemaphoreType.DMA((tp_count + dp_count,)),
         ],
         compiler_params=pltpu.CompilerParams(
             vmem_limit_bytes=VMEM_CAP, collective_id=2, has_side_effects=True
         ),
         cost_estimate=cost(87),
         name="final_step",
-    )(
-        query_grad, key_part, value_part, normed, weight, low, attended, router_grad,
-        hidden, gains, gain_two, middle_grad, middle, picker, bias, *outs,
-    )
+    )(key_part, value_part, gains, gain_two, bias, *late, *outs)
 
 
 def adam_kernel(*refs):
@@ -1372,7 +1458,8 @@
 
 def adam(weight, first, second, kept, arrived, far):
     count, rows, columns = weight.shape
-    step = max(size for size in range(16, rows + 1, 16) if rows % size == 0 and size * columns <= 1 << 17)
+    sizes = [size for size in range(16, rows + 1, 16) if rows % size == 0]
+    step = max(k for k in sizes if k * columns <= 400000 and count * rows >= 2 * k)
     plain = pl.BlockSpec((1, step, columns), lambda i, j: (i, j, 0))
     shape = jax.ShapeDtypeStruct(weight.shape, F32)
     return pl.pallas_call(
@@ -1504,11 +1591,13 @@
         out_own, grads_own, arrived, expert_in[0], expert_land, expert_down[0], expert_count,
     )
     middle, router_grad, middle_grad, middle_low, attended_grad, gain_two_grad = results[:6]
-    out_parts, results = results[6 : 6 + tp_count], results[6 + tp_count :]
+    out_sums, results = results[6 : 4 + dp_count], results[4 + dp_count :]
+    near_parts, results = results[:tp_count], results[tp_count:]
     attended, in_keep, in_core, in_sum, down_keep, down_core, down_far = results
 
     in_far = swap(in_sum, "ctx", 2)
-    out_far = [swap(out_parts[k], "tp", k) for k in range(1, tp_count)]
+    out_far = [swap(near_parts[k], "tp", k) for k in range(1, tp_count)]
+    out_far += [swap(out_sums[m - 2], "dp", m) for m in range(2, dp_count)]
     query_grad, key_part, value_part, bias_part = attention_back(
         info, queries, key_values, attended_grad, totals, position_bias, table, doc_row, doc_col
     )
@@ -1516,7 +1605,7 @@
     input_grad, output, bias_total, first_total, second_total, tail_total = final_step(
         query_grad, key_part, value_part, normed_flip, qkv_flat, middle_low, attended,
         router_grad, hidden_in, gains, gain_two_grad, middle_grad, middle, picker_flip, bias_part,
-        [out_parts[0]] + out_far, expert_count,
+        [near_parts[0]] + out_far, expert_count,
     )
     qkv_all, out_new, router_new, gains_new, bias_new = small_adam(
         first_total, second_total, tail_total, bias_total,

time: 389 us -> 371 us (0.954)
  the two profiles are of different devices: /device:TPU:0 before, /device:TPU:8 now
where the time goes in v1:
time: 371 us; the launch traced here: 364 us
  Pallas kernels  339 us (91%)
  starting transfers between devices  15.1 us (4%)
  local copies, waits for them, and re-layouts  7.02 us (2%)
    pallas_call x1, Pallas kernels, expert_step(): pl.pallas_call(functools.partial(expert_kernel, experts, dp_count, ctx_co...  120 us
    pallas_call x1, Pallas kernels, start(): pl.pallas_call(functools.partial(start_kernel, experts, dp_count, ctx_cou...  68.5 us
    pallas_call x1, Pallas kernels, final_step(): pl.pallas_call(functools.partial(final_kernel, experts, dp_count, ctx_cou...  66.4 us
    pallas_call x1, Pallas kernels, attention_back(): pl.pallas_call(attention_back_kernel, grid=(pairs,), in_specs=[specs['inf...  41.1 us
    pallas_call x2, Pallas kernels, attention(): pl.pallas_call(functools.partial(attention_kernel, first), grid=(count,),...  27.2 us
    ppermute x7, starting transfers between devices, swap(): return lax.ppermute(values, axis, [(i, i ^ bits) for i in range(count)])  15.1 us
    pallas_call x2, Pallas kernels, adam(): pl.pallas_call(adam_kernel, grid=(count, rows // step), in_specs=[plain]...  12.5 us
  transfers between devices with their start and end apart: 7, of which 2 were waited for; matrix products, arithmetic and copies ran while one was open for 0% of the time, Pallas kernels for 16%

profile of v1, /device:TPU:8, one launch (start us, length us, event | category | flops | bytes accessed | tf_op | source)
XLA Modules:
  0.0 363.8 jit_solution(16055577037247143546)
XLA Ops:
  0.7 0.8 reverse
  1.5 0.1 slice.10
  1.5 0.1 pad_dynamic-slice_fusion
  1.6 68.5 %start.1 = (bf16[512,512]{1,0:T(8,128)(2,1)}, bf16[2048,1024]{1,0:T(8,128)(2,1)}, bf16[1024,512]{1,0:T(8,128)(2,1)}, bf16[1024,1536]{1,0:T(8,128)(2,1)}, bf16[10...) custom-call(bf16[3,64,512]{2,1,0:T(8,128)(2,1)} %bitcast.48, ...), custom_call_target="tpu_custom_call" | custom-call | flops 69000003584 | bytes 1048576 | tf_op jit(solution)/shard_map/start/pallas_call | solution.py:692
  70.2 0.6 broadcast_in_dim.27.table_ref
  70.8 0.0 copy-start.2
  70.8 13.9 %attention_forward.2 = (bf16[512,256]{1,0:T(8,128)(2,1)}, f32[4,8,512]{2,1,0:T(8,128)}) custom-call(s32[8,128]{1,0:T(8,128)} %get-tuple-element.110.info_ref, bf16[512,512]{1,0:T(8,128)(2,1)} %get-tuple-element.111.query_ref, bf16[2048,1024]{1,0:T(8,128)(2,1)} %get-tuple-element.112.key_ref.value_ref, ...), custom_call_target="tpu_custom_call" | custom-call | flops 5750000128 | bytes 1048576 | tf_op jit(solution)/shard_map/attention_forward/pallas_call | solution.py:405
  84.7 0.5 collective-permute-start
  85.2 0.0 copy-done.2
  85.2 0.1 collective-permute-start.2
  85.3 2.7 collective-permute-start.1
  88.0 13.4 %attention_forward.3 = (bf16[512,256]{1,0:T(8,128)(2,1)}, f32[4,8,512]{2,1,0:T(8,128)}) custom-call(s32[8,128]{1,0:T(8,128)} %get-tuple-element.110.info_ref, bf16[512,512]{1,0:T(8,128)(2,1)} %get-tuple-element.111.query_ref, bf16[2048,1024]{1,0:T(8,128)(2,1)} %get-tuple-element.112.key_ref.value_ref, ...), custom_call_target="tpu_custom_call", output_to_operand_aliasing={{1}: (8, {})} | custom-call | flops 5750000128 | bytes 1048576 | tf_op jit(solution)/shard_map/attention_forward/pallas_call | solution.py:405
  101.4 0.0 collective-permute-done.refs_1_
  101.4 0.0 copy-start.9
  101.4 0.7 collective-permute-done.2.refs_6_
  102.1 0.0 copy-start.7
  102.1 1.0 collective-permute-done.1.refs_4_
  103.1 0.0 copy-start.8
  103.1 0.0 copy-done.9
  103.1 0.0 copy-done.7
  103.1 0.7 copy-done.8
  103.8 119.9 %expert_step.1 = (f32[512,1024]{1,0:T(8,128)}, f32[1024,128]{1,0:T(8,128)}, f32[512,1024]{1,0:T(8,128)}, bf16[512,1024]{1,0:T(8,128)(2,1)}, bf16[512,512]{1,0:T(...) custom-call(bf16[512,256]{1,0:T(8,128)(2,1)} %get-tuple-element.116., ...), custom_call_target="tpu_custom_call" | custom-call | flops 138000007168 | bytes 1048576 | tf_op jit(solution)/shard_map/expert_step/pallas_call | solution.py:1072
  223.7 8.1 %collective-permute-start.5 = (bf16[320,512]{1,0:T(8,128)(2,1)}, bf16[320,512]{1,0:T(8,128)(2,1)S(1)}, u32[]{:S(2)}, u32[]{:S(2)}) collective-permute-start(bf16[320,512]{1,0:T(8,128)(2,1)} %get-tuple-element.136), channel_id=1, source_target_pairs={{0,16},{8,24},{16,0},{24,8},{1,17},{9,25},{17,1},{25,9},{2,18},{10... | collective-permute-start | bytes 983048 | tf_op jit(solution)/shard_map/ppermute | solution.py:66
  231.8 1.8 collective-permute-start.6
  233.6 0.0 collective-permute-start.4
  233.6 1.8 collective-permute-start.3
  235.5 41.1 %attention_backward.1 = (bf16[512,512]{1,0:T(8,128)(2,1)}, bf16[2048,512]{1,0:T(8,128)(2,1)}, bf16[2048,512]{1,0:T(8,128)(2,1)}, f32[4,8,32]{2,1,0:T(8,128)}) custom-call(s32[8,128]{1,0:T(8,128)} %get-tuple-element.110.info_ref, bf16[512,512]{1,0:T(8,128)(2,1)} %get-tuple-element.111.query_ref, bf16[2048,1024]{1,0:T(8,128)(2,1)} %get-tuple-element.112.key_ref.value_ref, ...), custom_call_target="tpu_custom_call" | custom-call | flops 46000001024 | bytes 1048576 | tf_op jit(solution)/shard_map/attention_backward/pallas_call | solution.py:437
  276.6 4.7 %adam.3 = (f32[1,1408,256]{2,1,0:T(8,128)}, f32[1,1408,256]{2,1,0:T(8,128)}, f32[1,1408,256]{2,1,0:T(8,128)}, f32[1,1408,256]{2,1,0:T(8,128)}) custom-call(bf16[1,1408,256]{2,1,0:T(8,128)(2,1)} %refs_0_.1, f32[1,1408,256]{2,1,0:T(8,128)} %refs_1_.1, f32[1,1408,256]{2,1,0:T(8,128)} %refs_2_.1, bf16[1,1408,256]{2,1,0:T(8,128)(2,1)} %bitcast.63, ...), custom_call_target="tpu_custom_call" | custom-call | flops 5750000128 | bytes 1048576 | tf_op jit(solution)/shard_map/adam/pallas_call | solution.py:1465
  281.3 0.0 collective-permute-done.5.refs_12_
  281.3 0.0 copy-start.5
  281.3 0.0 collective-permute-done.6.refs_13_
  281.3 0.0 copy-start.6
  281.3 0.0 collective-permute-done.4.refs_11_
  281.3 0.0 copy-start.4
  281.3 0.0 collective-permute-done.3.refs_5_
  281.4 0.0 copy-start.3
  281.4 0.6 copy-done.5
  282.0 0.1 copy-done.6
  282.1 0.2 copy-done.4
  282.3 66.4 %final_step.1 = (f32[512,1024]{1,0:T(8,128)}, f32[512,1024]{1,0:T(8,128)}, f32[4,8,32]{2,1,0:T(8,128)}, f32[64,1024]{1,0:T(8,128)}, f32[64,1024]{1,0:T(8,128)}, /*index=5*/f32[128,128]{1,0:T(8,128)}) custom-call(bf16[2048,512]{1,0:T(8,128)(2,1)} %get-tuple-element.129.key_ref, bf16[2048,512]{1,0:T(8,128)(2,1)} %get-tuple-element.130.value_ref, ...), custom_call_target="tpu_custom_call" | custom-call | flops 100050001920 | bytes 1048576 | tf_op jit(solution)/shard_map/final_step/pallas_call | solution.py:1398
  348.8 0.0 copy-done.3
  348.8 7.8 %adam.2 = (f32[2,256,1408]{2,1,0:T(8,128)}, f32[2,256,1408]{2,1,0:T(8,128)}, f32[2,256,1408]{2,1,0:T(8,128)}, f32[2,256,1408]{2,1,0:T(8,128)}) custom-call(bf16[2,256,1408]{2,1,0:T(8,128)(2,1)} %bitcast.44, f32[2,256,1408]{2,1,0:T(8,128)} %bitcast.40, f32[2,256,1408]{2,1,0:T(8,128)} %bitcast.41, bf16[2,256,1408]{2,1,0:T(8,128)(2,1)} %get-tuple-element.176.refs_3_, ...), custom_call_target="tpu_custom_call" | custom-call | flops 5750000128 | bytes 1048576 | tf_op jit(solution)/shard_map/adam/pallas_call | solution.py:1465
  356.6 3.3 small_adam.1
  359.9 0.0 copy-done.1
  359.9 0.0 copy-start
  359.9 1.3 copy.60
  361.2 1.0 copy-done
  362.2 1.3 copy.61
  (2 shorter events, 0.0 us)
Async XLA Ops:
  70.8 14.4 %copy-start.2 = (bf16[3,320,512]{2,1,0:T(8,128)(2,1)S(1)}, bf16[3,320,512]{2,1,0:T(8,128)(2,1)}, u32[]{:S(2)}) copy-start(bf16[3,320,512]{2,1,0:T(8,128)(2,1)} %get-tuple-element.124) | copy-start | bytes 2949124
  84.7 16.7 %collective-permute-start = (bf16[512,256]{1,0:T(8,128)(2,1)}, bf16[512,256]{1,0:T(8,128)(2,1)S(1)}, u32[]{:S(2)}, u32[]{:S(2)}) collective-permute-start(bf16[512,256]{1,0:T(8,128)(2,1)} %get-tuple-element.121.refs_0_), channel_id=1, source_target_pairs={{0,1},{1,0},{2,3},{3,2},{4,5},{5,4},{6,7},{7,6},{8,9},{9,8},{10,11... | collective-permute-start | bytes 786440 | tf_op jit(solution)/shard_map/ppermute | solution.py:66
  85.2 16.9 %collective-permute-start.2 = (bf16[320,512]{1,0:T(8,128)(2,1)S(1)}, bf16[320,512]{1,0:T(8,128)(2,1)S(1)}, u32[]{:S(2)}, u32[]{:S(2)}) collective-permute-start(bf16[320,512]{1,0:T(8,128)(2,1)S(1)} %get-tuple-element.190), channel_id=1, source_target_pairs={{0,24},{8,16},{16,8},{24,0},{1,25},{9,17},{17,9},{25,1},{2,26},{10... | collective-permute-start | bytes 983048 | tf_op jit(solution)/shard_map/ppermute | solution.py:66
  85.3 17.8 %collective-permute-start.1 = (bf16[320,512]{1,0:T(8,128)(2,1)S(1)}, bf16[320,512]{1,0:T(8,128)(2,1)S(1)}, u32[]{:S(2)}, u32[]{:S(2)}) collective-permute-start(bf16[320,512]{1,0:T(8,128)(2,1)S(1)} %get-tuple-element.191), channel_id=1, source_target_pairs={{0,8},{8,0},{16,24},{24,16},{1,9},{9,1},{17,25},{25,17},{2,10},{10... | collective-permute-start | bytes 983048 | tf_op jit(solution)/shard_map/ppermute | solution.py:66
  101.4 1.7 copy-start.9
  102.1 1.0 copy-start.7
  103.1 0.7 copy-start.8
  223.7 57.6 %collective-permute-start.5 = (bf16[320,512]{1,0:T(8,128)(2,1)}, bf16[320,512]{1,0:T(8,128)(2,1)S(1)}, u32[]{:S(2)}, u32[]{:S(2)}) collective-permute-start(bf16[320,512]{1,0:T(8,128)(2,1)} %get-tuple-element.136), channel_id=1, source_target_pairs={{0,16},{8,24},{16,0},{24,8},{1,17},{9,25},{17,1},{25,9},{2,18},{10... | collective-permute-start | bytes 983048 | tf_op jit(solution)/shard_map/ppermute | solution.py:66
  231.8 49.5 %collective-permute-start.6 = (bf16[320,512]{1,0:T(8,128)(2,1)}, bf16[320,512]{1,0:T(8,128)(2,1)S(1)}, u32[]{:S(2)}, u32[]{:S(2)}) collective-permute-start(bf16[320,512]{1,0:T(8,128)(2,1)} %get-tuple-element.137), channel_id=1, source_target_pairs={{0,24},{8,16},{16,8},{24,0},{1,25},{9,17},{17,9},{25,1},{2,26},{10... | collective-permute-start | bytes 983048 | tf_op jit(solution)/shard_map/ppermute | solution.py:66
  233.6 47.7 %collective-permute-start.4 = (bf16[2,320,512]{2,1,0:T(8,128)(2,1)}, bf16[2,320,512]{2,1,0:T(8,128)(2,1)S(1)}, u32[]{:S(2)}, u32[]{:S(2)}) collective-permute-start(bf16[2,320,512]{2,1,0:T(8,128)(2,1)} %get-tuple-element.135), channel_id=1, source_target_pairs={{0,1},{1,0},{2,3},{3,2},{4,5},{5,4},{6,7},{7,6},{8,9},{9,8},{10,11... | collective-permute-start | bytes 1966088 | tf_op jit(solution)/shard_map/ppermute | solution.py:66
  233.6 47.7 %collective-permute-start.3 = (bf16[2,256,1408]{2,1,0:T(8,128)(2,1)}, bf16[2,256,1408]{2,1,0:T(8,128)(2,1)S(1)}, u32[]{:S(2)}, u32[]{:S(2)}) collective-permute-start(bf16[2,256,1408]{2,1,0:T(8,128)(2,1)} %get-tuple-element.134), channel_id=1, source_target_pairs={{0,4},{2,6},{4,0},{6,2},{1,5},{3,7},{5,1},{7,3},{8,12},{10,14},{12... | collective-permute-start | bytes 4325384 | tf_op jit(solution)/shard_map/ppermute | solution.py:66
  281.3 0.7 copy-start.5
  281.3 0.8 copy-start.6
  281.3 1.0 copy-start.4
  281.4 67.4 %copy-start.3 = (bf16[2,256,1408]{2,1,0:T(8,128)(2,1)}, bf16[2,256,1408]{2,1,0:T(8,128)(2,1)S(1)}, u32[]{:S(2)}) copy-start(bf16[2,256,1408]{2,1,0:T(8,128)(2,1)S(1)} %collective-permute-done.3.refs_5_) | copy-start | bytes 4325380
  356.6 3.3 copy-start.1
  359.9 2.3 copy-start

commit v2 on v1

--- a/solution.py
+++ b/solution.py
@@ -26,6 +26,7 @@
 BF16 = jnp.bfloat16
 LANES = 128
 BLOCK = 256
+FF_STEP = 256
 VMEM_CAP = 60 * 1024 * 1024
 GELU_K = 0.7978845608028654
 GELU_C = 0.044715
@@ -467,16 +468,26 @@
 
 def start_kernel(
     experts, dp_count, ctx_count, tp_count, qkv_ref, out_flip_ref, router_ref, gain_pair_ref,
-    hidden_ref, segments_ref, routes_ref, out_grad_ref, expert_ref,
-    query_ref, pair_ref, normed_flip_ref, weight_out, own_ref, lanes_ref, gains_ref, info_ref,
-    row_ref, column_ref, picker_ref, picker_rows_ref, grads_own_ref, grads_ref, early_land,
+    hidden_ref, segments_ref, routes_ref, out_grad_hbm, expert_ref,
+    query_ref, pair_out, normed_flip_ref, weight_out, own_ref, lanes_ref, gains_ref, info_ref,
+    row_ref, column_out, picker_out, picker_rows_out, grads_own_out, grads_out, early_land,
     expert_land,
-    weights, out_all, hidden, docs, docs_ref, flip, sends, receives, out_sem,
+    weights, out_all, hidden, docs, docs_ref, flip, pair_ref, column_ref, picker_ref,
+    picker_rows_ref, grads_own_ref, grads_ref, out_grad_ref, sends, receives, out_sem, in_sem,
 ):
     d, c, t = lax.axis_index("dp"), lax.axis_index("ctx"), lax.axis_index("tp")
     rows = out_flip_ref.shape[0]
     tokens, width = query_ref.shape
     early = early_blocks(dp_count)
+    out_grad_load = pltpu.make_async_copy(out_grad_hbm, out_grad_ref, in_sem)
+    out_grad_load.start()
+    stores = []
+
+    def store(source, target):
+        copy = pltpu.make_async_copy(source, target, out_sem.at[len(stores)])
+        copy.start()
+        stores.append(copy)
+
     own_rows = pl.ds(pl.multiple_of((d * ctx_count + c) * rows, rows), rows)
     own_lanes = pl.ds(pl.multiple_of(t * width, width), width)
     for part in range(3):
@@ -575,12 +586,18 @@
     hidden_sent[2].wait()
     half = hidden.at[2, :, own_share]
     spread = [wire.send(half, half, tp=t ^ k) for k in range(1, tp_count)]
+    out_grad_load.wait()
     for m in range(dp_count):
         chosen = picker_rows_ref[m * slots : (m + 1) * slots, :]
         if m:
             grads_ref[m - 1] = mm(chosen, out_grad_ref[:, own_share]).astype(BF16)
         else:
             grads_own_ref[...] = mm(chosen, out_grad_ref[...]).astype(BF16)
+
+    store(picker_ref, picker_out)
+    store(picker_rows_ref, picker_rows_out)
+    store(grads_own_ref, grads_own_out)
+    store(grads_ref, grads_out)
 
     key_blocks, query_blocks = tokens // BLOCK, tokens // BLOCK
     where = lax.broadcasted_iota(jnp.int32, info_ref.shape, 1)
@@ -614,6 +631,7 @@
         steps = lax.shift_right_logical(count + 1, 1)
         info = jnp.where(which == query_blocks + q, steps, info)
     info_ref[...] = info
+    store(column_ref, column_out)
 
     early_copies = []
     for i, m in enumerate(order[1:]):
@@ -634,8 +652,7 @@
     hidden_sent[3] = wire.send(hidden.at[2], hidden.at[3], ctx=c ^ 1)
     for copy in crossed[0]:
         copy.wait()
-    keep = pltpu.make_async_copy(weights.at[:, : 3 * width], weight_out, out_sem.at[0])
-    keep.start()
+    store(weights.at[:, : 3 * width], weight_out)
     small = weights[:, 3 * width : 3 * width + LANES].astype(F32)
     lane = lax.broadcasted_iota(jnp.int32, small.shape, 1)
     lanes_ref[...] = jnp.where(lane < experts, small, 0.0).astype(BF16)
@@ -653,6 +670,8 @@
         pair_ref[m * tokens : (m + 1) * tokens, :] = mm(
             normed, weights[:, width : 3 * width]
         ).astype(BF16)
+        here = pl.ds(m * tokens, tokens)
+        store(pair_ref.at[here], pair_out.at[here])
         if m == 0:
             normed_flip_ref[...] = normed.T
             query_ref[...] = mm(normed, weights[:, :width]).astype(BF16)
@@ -663,8 +682,7 @@
                 crossed[1] += [send_shard(n, j, 1, lanes, ctx=c ^ 1) for j in sides]
     for copy in crossed[1]:
         copy.wait()
-    keep_own = pltpu.make_async_copy(out_all, own_ref, out_sem.at[1])
-    keep_own.start()
+    store(out_all, own_ref)
     for k in [k for k in expert_sent if k > 1]:
         expert_sent[k].wait()
         expert_sent[k | 1] = wire.send(expert_land.at[k - 1], expert_land.at[k], ctx=c ^ 1)
@@ -672,8 +690,8 @@
         expert_sent[k].wait()
     for copy in early_copies:
         copy.wait()
-    keep.wait()
-    keep_own.wait()
+    for copy in stores:
+        copy.wait()
     wire.finish()
 
 
@@ -691,8 +709,8 @@
     shape = jax.ShapeDtypeStruct
     return pl.pallas_call(
         functools.partial(start_kernel, experts, dp_count, ctx_count, tp_count),
-        in_specs=[vmem] * 8 + [hbm],
-        out_specs=[vmem] * 3 + [hbm] * 2 + [vmem] * 9 + [hbm] * 2,
+        in_specs=[vmem] * 7 + [hbm] * 2,
+        out_specs=[vmem, hbm, vmem] + [hbm] * 2 + [vmem] * 4 + [hbm] * 7,
         out_shape=[
             shape((tokens, width), BF16),
             shape((tokens * ctx_count, 2 * width), BF16),
@@ -718,9 +736,17 @@
             pltpu.VMEM((ctx_count, 8, tokens), jnp.int32),
             pltpu.VMEM((8, tokens), jnp.int32),
             pltpu.VMEM((LANES, tokens), F32),
+            pltpu.VMEM((tokens * ctx_count, 2 * width), BF16),
+            pltpu.VMEM((tokens * ctx_count, LANES), jnp.int32),
+            pltpu.VMEM((tokens, dp_count * slots), BF16),
+            pltpu.VMEM((dp_count * slots, tokens), BF16),
+            pltpu.VMEM((slots, D), BF16),
+            pltpu.VMEM((dp_count - 1, slots, D // tp_count), BF16),
+            pltpu.VMEM((tokens, D), BF16),
             pltpu.SemaphoreType.DMA((copies,)),
             pltpu.SemaphoreType.DMA((copies,)),
-            pltpu.SemaphoreType.DMA((2,)),
+            pltpu.SemaphoreType.DMA((7 + ctx_count,)),
+            pltpu.SemaphoreType.DMA(()),
         ],
         compiler_params=pltpu.CompilerParams(
             vmem_limit_bytes=VMEM_CAP, collective_id=1, has_side_effects=True
@@ -749,14 +775,14 @@
     in_own, in_land, refs = refs[0], refs[1], refs[2:]
     ins = [in_own] + [in_land.at[j] for j in range(ctx_count - 1)]
     down_own, refs = refs[0], refs[1:]
-    middle_ref, router_grad_ref, grad_ref, low_ref, attended_grad_ref, gain_ref = refs[:6]
+    middle_out, router_grad_ref, grad_ref, low_ref, attended_grad_ref, gain_ref = refs[:6]
     out_sums, refs = refs[6 : 4 + dp_count], refs[4 + dp_count :]
     near_parts, refs = refs[:tp_count], refs[tp_count:]
     (attended_out, in_keep, in_core, in_sum, down_keep, down_core, down_far,
      mixed, out_all, in_all, down_all, rows_all, scaled_all, act_all, gate_all, up_all, send_rows,
      row_parts, row_in, row_back, dot_parts, dot_in, dot_home, dot_back, probs, whole,
      normed_flip, in_land_far, down_land_far, out_parts, out_in, hidden_ref, out_grad_ref,
-     picker_ref, picker_rows_ref, sends, receives, in_sems, keep_sems) = refs
+     picker_ref, picker_rows_ref, middle_ref, sends, receives, in_sems, keep_sems) = refs
     tokens, second_width = attended_ref.shape
     first_width = firsts[0].shape[1]
     width = first_width + second_width
@@ -773,6 +799,13 @@
         copy.start()
         local.append(copy)
         return copy
+
+    keeps = []
+
+    def keep(source, target):
+        copy = pltpu.make_async_copy(source, target, keep_sems.at[len(keeps)])
+        copy.start()
+        keeps.append(copy)
 
     out_copies = [
         load(out_ref, out_all),
@@ -799,7 +832,7 @@
     for m in range(tp_count):
         start = pl.multiple_of((t ^ m) * width, width)
         mixed[:, pl.ds(start, first_width)] = firsts[m][...]
-    attended_out[...] = mixed[:, own_lanes]
+    keep(mixed.at[:, own_lanes], attended_out)
     greet(
         [{"tp": t ^ k} for k in shares]
         + [{"dp": d ^ m} for m in range(1, dp_count)]
@@ -826,20 +859,28 @@
         copy.wait()
     middle = hidden_ref[...].astype(F32) + mm(mixed[...], out_all[...], NT)
     middle_ref[...] = middle
+    keep(middle_ref, middle_out)
     scale = lax.rsqrt(jnp.mean(middle * middle, axis=-1, keepdims=True) + NORM_EPS)
     normed = (middle * scale * gains_ref[1:2, :]).astype(BF16)
     far = {}
+    cut = slots // 2 if slots % 32 == 0 else slots
 
     def block(m):
         return slice(m * slots, (m + 1) * slots)
+
+    def pieces(m):
+        return [slice(m * slots + k, m * slots + k + cut) for k in range(0, slots, cut)]
 
     for m in order[1:] + [0]:
         picked = mm(picker_rows_ref[block(m), :], normed).astype(BF16)
         if m:
             send_rows[m - 1] = picked
-            far[m] = wire.send(
-                send_rows.at[m - 1, :, own_share], rows_all.at[block(m), own_share], dp=d ^ m
-            )
+            far[m] = [
+                wire.send(
+                    send_rows.at[m - 1, here, own_share], rows_all.at[there, own_share], dp=d ^ m
+                )
+                for here, there in zip(pieces(0), pieces(m))
+            ]
         else:
             rows_all[block(0), :] = picked
     lane = lax.broadcasted_iota(jnp.int32, (tokens, LANES), 1)
@@ -864,9 +905,10 @@
     gates = {}
 
     def forward(m):
-        far[m].wait()
-        half = rows_all.at[block(m), own_share]
-        spread[m] += [wire.send(half, half, tp=t ^ k) for k in shares]
+        for copy, piece in zip(far[m], pieces(m)):
+            copy.wait()
+            half = rows_all.at[piece, own_share]
+            spread[m] += [wire.send(half, half, tp=t ^ k) for k in shares]
 
     def experts_on(m, hook):
         here = block(m)
@@ -877,8 +919,8 @@
         rows_all[here, :] = rows
         scaled_all[here, :] = (gate * grad_rows.astype(F32)).astype(BF16)
         dots = jnp.zeros((slots, LANES), F32)
-        for first in range(0, ff, BLOCK):
-            part = slice(first, min(ff, first + BLOCK))
+        for first in range(0, ff, FF_STEP):
+            part = slice(first, min(ff, first + FF_STEP))
             value = mm(rows, in_all[0, :, part])
             up = mm(rows, in_all[1, :, part])
             back = mm(grad_rows, down_all[part, :], NT)
@@ -904,7 +946,10 @@
                 row_parts[k, m, :, i * depth : (i + 1) * depth] = row.astype(BF16)
             if k:
                 returned.setdefault(m, []).append(
-                    wire.send(row_parts.at[k, m], row_in.at[k - 1, m], tp=t ^ k)
+                    [
+                        wire.send(row_parts.at[k, m, here], row_in.at[k - 1, m, here], tp=t ^ k)
+                        for here in pieces(0)
+                    ]
                 )
         gates[m] = gate
 
@@ -918,24 +963,27 @@
                     gates[m] * mm(act_all[here, :], down_all[:, part])
                 ).astype(BF16)
 
-    homeward = []
+    homeward, dots_homeward = [], []
 
     def send_home(m):
         for copy in dot_returned[m]:
             copy.wait()
         dots = tree_sum([dot_parts[m]] + [dot_in[k - 1, m] for k in shares])
-        total = row_parts[0, m].astype(F32)
-        for k, copy in zip(shares, returned[m]):
-            copy.wait()
-            total = total + row_in[k - 1, m].astype(F32)
         if m:
             dot_home[m] = dots
-            row_parts[0, m] = total.astype(BF16)
-            homeward.append(wire.send(dot_home.at[m], dot_back.at[m], dp=d ^ m))
-            homeward.append(wire.send(row_parts.at[0, m], row_back.at[block(m)], dp=d ^ m))
+            dots_homeward.append(wire.send(dot_home.at[m], dot_back.at[m], dp=d ^ m))
         else:
             dot_back[0] = dots
-            row_back[block(0), :] = total.astype(BF16)
+        for i, (here, there) in enumerate(zip(pieces(0), pieces(m))):
+            total = row_parts[0, m, here].astype(F32)
+            for k, copies in zip(shares, returned[m]):
+                copies[i].wait()
+                total = total + row_in[k - 1, m, here].astype(F32)
+            if m:
+                row_parts[0, m, here] = total.astype(BF16)
+                homeward.append(wire.send(row_parts.at[0, m, here], row_back.at[there], dp=d ^ m))
+            else:
+                row_back[there, :] = total.astype(BF16)
 
     for i, m in enumerate(order):
         for copy in spread.get(m, []):
@@ -951,13 +999,6 @@
         for side, right in enumerate((gate_all, up_all)):
             in_all[side, part, :] = mm(rows_all[:, part], right[...], TN).astype(BF16)
 
-    keeps = []
-
-    def keep(source, target):
-        copy = pltpu.make_async_copy(source, target, keep_sems.at[len(keeps)])
-        copy.start()
-        keeps.append(copy)
-
     def part_of(j):
         return slice(j * depth, (j + 1) * depth)
 
@@ -969,7 +1010,7 @@
         for k in shares
     ]
     for k in range(tp_count):
-        near_parts[k][...] = out_parts[k, :2]
+        keep(out_parts.at[k, :2], near_parts[k])
     downs[3].sent()
     for first in range(0, ff, BLOCK):
         part = slice(first, min(ff, first + BLOCK))
@@ -999,9 +1040,8 @@
     in_grads(0)
     keep(in_all.at[:, part_of(0), :], in_keep)
 
-    for copy in homeward:
-        copy.wait()
-    result = mm(picker_ref[...], row_back[...])
+    for copy in dots_homeward:
+        copy.wait()
     prob_grad = jnp.zeros((tokens, LANES), F32)
     for m in range(dp_count):
         high = dot_back[m].astype(BF16)
@@ -1018,6 +1058,9 @@
         logit, lanes_ref[own_share, :].astype(F32), NT, precision=lax.Precision.HIGHEST,
         preferred_element_type=F32,
     )
+    for copy in homeward:
+        copy.wait()
+    result = mm(picker_ref[...], row_back[...])
     whole[:, own_share] = (result + more).astype(BF16)
     arrivals = [wire.send(whole.at[:, own_share], whole.at[:, own_share], tp=t ^ k) for k in shares]
     logit_high = logit.astype(BF16)
@@ -1065,14 +1108,14 @@
     depth, ff = expert.shape[1], expert.shape[2]
     all_slots = dp_count * slots
     others = tp_count - 1
-    copies = others * (2 + 5 * dp_count) + 3 * dp_count + 8
+    copies = others * (2 + 8 * dp_count) + 5 * dp_count + 8
     vmem = pl.BlockSpec(memory_space=pltpu.VMEM)
     hbm = pl.BlockSpec(memory_space=pl.ANY)
     shape = jax.ShapeDtypeStruct
     return pl.pallas_call(
         functools.partial(expert_kernel, experts, dp_count, ctx_count, tp_count),
         in_specs=[vmem] * 3 + [hbm] * 4 + [vmem] * tp_count + [hbm] * (4 + dp_count),
-        out_specs=[vmem] * (5 + dp_count + tp_count) + [hbm] * 6,
+        out_specs=[hbm] + [vmem] * (3 + dp_count) + [hbm] * (tp_count + 7),
         out_shape=[
             shape((tokens, D), F32),
             shape((D, LANES), F32),
@@ -1115,10 +1158,11 @@
             pltpu.VMEM((tokens, D), BF16),
             pltpu.VMEM((tokens, all_slots), BF16),
             pltpu.VMEM((all_slots, tokens), BF16),
+            pltpu.VMEM((tokens, D), F32),
             pltpu.SemaphoreType.DMA((copies,)),
             pltpu.SemaphoreType.DMA((copies,)),
             pltpu.SemaphoreType.DMA((6 + ctx_count + dp_count,)),
-            pltpu.SemaphoreType.DMA((3,)),
+            pltpu.SemaphoreType.DMA((5 + tp_count,)),
         ],
         compiler_params=pltpu.CompilerParams(
             vmem_limit_bytes=VMEM_CAP, collective_id=3, has_side_effects=True

time: 371 us -> 359 us (0.968)
  the two profiles are of different devices: /device:TPU:8 before, /device:TPU:0 now
where the time goes in v2:
time: 359 us; the launch traced here: 353 us
  Pallas kernels  335 us (93%)
  local copies, waits for them, and re-layouts  7.02 us (2%)
  waiting for transfers between devices  4.86 us (1%)
  starting transfers between devices  4.78 us (1%)
    pallas_call x1, Pallas kernels, expert_step(): pl.pallas_call(functools.partial(expert_kernel, experts, dp_count, ctx_co...  122 us
    pallas_call x1, Pallas kernels, start(): pl.pallas_call(functools.partial(start_kernel, experts, dp_count, ctx_cou...  71.4 us
    pallas_call x1, Pallas kernels, final_step(): pl.pallas_call(functools.partial(final_kernel, experts, dp_count, ctx_cou...  71.1 us
    pallas_call x1, Pallas kernels, attention_back(): pl.pallas_call(attention_back_kernel, grid=(pairs,), in_specs=[specs['inf...  32.9 us
    pallas_call x2, Pallas kernels, attention(): pl.pallas_call(functools.partial(attention_kernel, first), grid=(count,),...  22.5 us
    pallas_call x2, Pallas kernels, adam(): pl.pallas_call(adam_kernel, grid=(count, rows // step), in_specs=[plain]...  12.5 us
  transfers between devices with their start and end apart: 7, of which 1 were waited for; matrix products, arithmetic and copies ran while one was open for 0% of the time, Pallas kernels for 14%

profile of v2, /device:TPU:0, one launch (start us, length us, event | category | flops | bytes accessed | tf_op | source)
XLA Modules:
  0.0 353.1 jit_solution(17687140103716150124)
XLA Ops:
  0.7 0.8 reverse
  1.5 0.1 slice.10
  1.5 0.1 pad_dynamic-slice_fusion
  1.6 71.4 %start.1 = (bf16[512,512]{1,0:T(8,128)(2,1)}, bf16[2048,1024]{1,0:T(8,128)(2,1)}, bf16[1024,512]{1,0:T(8,128)(2,1)}, bf16[1024,1536]{1,0:T(8,128)(2,1)}, bf16[10...) custom-call(bf16[3,64,512]{2,1,0:T(8,128)(2,1)} %bitcast.48, ...), custom_call_target="tpu_custom_call" | custom-call | flops 69000003584 | bytes 1048576 | tf_op jit(solution)/shard_map/start/pallas_call | solution.py:710
  73.1 0.6 broadcast_in_dim.27.table_ref
  73.7 0.0 copy-start.2
  73.7 11.4 %attention_forward.2 = (bf16[512,256]{1,0:T(8,128)(2,1)}, f32[4,8,512]{2,1,0:T(8,128)}) custom-call(s32[8,128]{1,0:T(8,128)} %get-tuple-element.110.info_ref, bf16[512,512]{1,0:T(8,128)(2,1)} %get-tuple-element.111.query_ref, bf16[2048,1024]{1,0:T(8,128)(2,1)} %get-tuple-element.112.key_ref.value_ref, ...), custom_call_target="tpu_custom_call" | custom-call | flops 5750000128 | bytes 1048576 | tf_op jit(solution)/shard_map/attention_forward/pallas_call | solution.py:406
  85.2 0.5 collective-permute-start
  85.7 0.0 copy-done.2
  85.7 0.1 collective-permute-start.2
  85.8 0.1 collective-permute-start.1
  85.9 11.0 %attention_forward.3 = (bf16[512,256]{1,0:T(8,128)(2,1)}, f32[4,8,512]{2,1,0:T(8,128)}) custom-call(s32[8,128]{1,0:T(8,128)} %get-tuple-element.110.info_ref, bf16[512,512]{1,0:T(8,128)(2,1)} %get-tuple-element.111.query_ref, bf16[2048,1024]{1,0:T(8,128)(2,1)} %get-tuple-element.112.key_ref.value_ref, ...), custom_call_target="tpu_custom_call", output_to_operand_aliasing={{1}: (8, {})} | custom-call | flops 5750000128 | bytes 1048576 | tf_op jit(solution)/shard_map/attention_forward/pallas_call | solution.py:406
  96.9 0.0 collective-permute-done.refs_1_
  96.9 0.0 copy-start.9
  96.9 0.0 collective-permute-done.2.refs_6_
  96.9 0.0 copy-start.7
  96.9 4.8 %collective-permute-done.1.refs_4_ = bf16[320,512]{1,0:T(8,128)(2,1)S(1)} collective-permute-done((bf16[320,512]{1,0:T(8,128)(2,1)S(1)}, bf16[320,512]{1,0:T(8,128)(2,1)S(1)}, u32[]{:S(2)}, u32[]{:S(2)}) %collective-permute-start.1) | collective-permute-done | bytes 327712 | tf_op jit(solution)/shard_map/ppermute | solution.py:67
  101.8 0.0 copy-start.8
  101.8 0.0 copy-done.9
  101.8 0.0 copy-done.7
  101.8 0.7 copy-done.8
  102.5 121.6 %expert_step.1 = (f32[512,1024]{1,0:T(8,128)}, f32[1024,128]{1,0:T(8,128)}, f32[512,1024]{1,0:T(8,128)}, bf16[512,1024]{1,0:T(8,128)(2,1)}, bf16[512,512]{1,0:T(...) custom-call(bf16[512,256]{1,0:T(8,128)(2,1)} %get-tuple-element.116., ...), custom_call_target="tpu_custom_call" | custom-call | flops 138000007168 | bytes 1048576 | tf_op jit(solution)/shard_map/expert_step/pallas_call | solution.py:1115
  224.1 0.1 collective-permute-start.5
  224.2 3.5 collective-permute-start.6
  227.7 0.4 collective-permute-start.4
  228.1 0.2 collective-permute-start.3
  228.3 32.9 %attention_backward.1 = (bf16[512,512]{1,0:T(8,128)(2,1)}, bf16[2048,512]{1,0:T(8,128)(2,1)}, bf16[2048,512]{1,0:T(8,128)(2,1)}, f32[4,8,32]{2,1,0:T(8,128)}) custom-call(s32[8,128]{1,0:T(8,128)} %get-tuple-element.110.info_ref, bf16[512,512]{1,0:T(8,128)(2,1)} %get-tuple-element.111.query_ref, bf16[2048,1024]{1,0:T(8,128)(2,1)} %get-tuple-element.112.key_ref.value_ref, ...), custom_call_target="tpu_custom_call" | custom-call | flops 46000001024 | bytes 1048576 | tf_op jit(solution)/shard_map/attention_backward/pallas_call | solution.py:438
  261.1 4.7 %adam.3 = (f32[1,1408,256]{2,1,0:T(8,128)}, f32[1,1408,256]{2,1,0:T(8,128)}, f32[1,1408,256]{2,1,0:T(8,128)}, f32[1,1408,256]{2,1,0:T(8,128)}) custom-call(bf16[1,1408,256]{2,1,0:T(8,128)(2,1)} %refs_0_.1, f32[1,1408,256]{2,1,0:T(8,128)} %refs_1_.1, f32[1,1408,256]{2,1,0:T(8,128)} %refs_2_.1, bf16[1,1408,256]{2,1,0:T(8,128)(2,1)} %bitcast.63, ...), custom_call_target="tpu_custom_call" | custom-call | flops 5750000128 | bytes 1048576 | tf_op jit(solution)/shard_map/adam/pallas_call | solution.py:1509
  265.8 0.0 collective-permute-done.5.refs_12_
  265.8 0.0 copy-start.5
  265.9 0.0 collective-permute-done.6.refs_13_
  265.9 0.0 copy-start.6
  265.9 0.0 collective-permute-done.4.refs_11_
  265.9 0.0 copy-start.4
  265.9 0.0 collective-permute-done.3.refs_5_
  265.9 0.0 copy-start.3
  265.9 0.6 copy-done.5
  266.6 0.1 copy-done.6
  266.7 0.2 copy-done.4
  266.9 71.1 %final_step.1 = (f32[512,1024]{1,0:T(8,128)}, f32[512,1024]{1,0:T(8,128)}, f32[4,8,32]{2,1,0:T(8,128)}, f32[64,1024]{1,0:T(8,128)}, f32[64,1024]{1,0:T(8,128)}, /*index=5*/f32[128,128]{1,0:T(8,128)}) custom-call(bf16[2048,512]{1,0:T(8,128)(2,1)} %get-tuple-element.129.key_ref, bf16[2048,512]{1,0:T(8,128)(2,1)} %get-tuple-element.130.value_ref, ...), custom_call_target="tpu_custom_call" | custom-call | flops 100050001920 | bytes 1048576 | tf_op jit(solution)/shard_map/final_step/pallas_call | solution.py:1442
  338.1 0.0 copy-done.3
  338.1 7.8 %adam.2 = (f32[2,256,1408]{2,1,0:T(8,128)}, f32[2,256,1408]{2,1,0:T(8,128)}, f32[2,256,1408]{2,1,0:T(8,128)}, f32[2,256,1408]{2,1,0:T(8,128)}) custom-call(bf16[2,256,1408]{2,1,0:T(8,128)(2,1)} %bitcast.44, f32[2,256,1408]{2,1,0:T(8,128)} %bitcast.40, f32[2,256,1408]{2,1,0:T(8,128)} %bitcast.41, bf16[2,256,1408]{2,1,0:T(8,128)(2,1)} %get-tuple-element.176.refs_3_, ...), custom_call_target="tpu_custom_call" | custom-call | flops 5750000128 | bytes 1048576 | tf_op jit(solution)/shard_map/adam/pallas_call | solution.py:1509
  345.9 3.3 small_adam.1
  349.1 0.0 copy-done.1
  349.2 0.0 copy-start
  349.2 1.3 copy.60
  350.5 1.0 copy-done
  351.5 1.3 copy.61
  (2 shorter events, 0.0 us)
Async XLA Ops:
  73.7 11.9 %copy-start.2 = (bf16[3,320,512]{2,1,0:T(8,128)(2,1)S(1)}, bf16[3,320,512]{2,1,0:T(8,128)(2,1)}, u32[]{:S(2)}) copy-start(bf16[3,320,512]{2,1,0:T(8,128)(2,1)} %get-tuple-element.124) | copy-start | bytes 2949124
  85.2 11.7 %collective-permute-start = (bf16[512,256]{1,0:T(8,128)(2,1)}, bf16[512,256]{1,0:T(8,128)(2,1)S(1)}, u32[]{:S(2)}, u32[]{:S(2)}) collective-permute-start(bf16[512,256]{1,0:T(8,128)(2,1)} %get-tuple-element.121.refs_0_), channel_id=1, source_target_pairs={{0,1},{1,0},{2,3},{3,2},{4,5},{5,4},{6,7},{7,6},{8,9},{9,8},{10,11... | collective-permute-start | bytes 786440 | tf_op jit(solution)/shard_map/ppermute | solution.py:67
  85.7 11.2 %collective-permute-start.2 = (bf16[320,512]{1,0:T(8,128)(2,1)S(1)}, bf16[320,512]{1,0:T(8,128)(2,1)S(1)}, u32[]{:S(2)}, u32[]{:S(2)}) collective-permute-start(bf16[320,512]{1,0:T(8,128)(2,1)S(1)} %get-tuple-element.190), channel_id=1, source_target_pairs={{0,24},{8,16},{16,8},{24,0},{1,25},{9,17},{17,9},{25,1},{2,26},{10... | collective-permute-start | bytes 983048 | tf_op jit(solution)/shard_map/ppermute | solution.py:67
  85.8 16.0 %collective-permute-start.1 = (bf16[320,512]{1,0:T(8,128)(2,1)S(1)}, bf16[320,512]{1,0:T(8,128)(2,1)S(1)}, u32[]{:S(2)}, u32[]{:S(2)}) collective-permute-start(bf16[320,512]{1,0:T(8,128)(2,1)S(1)} %get-tuple-element.191), channel_id=1, source_target_pairs={{0,8},{8,0},{16,24},{24,16},{1,9},{9,1},{17,25},{25,17},{2,10},{10... | collective-permute-start | bytes 983048 | tf_op jit(solution)/shard_map/ppermute | solution.py:67
  96.9 4.9 %copy-start.9 = (bf16[512,256]{1,0:T(8,128)(2,1)}, bf16[512,256]{1,0:T(8,128)(2,1)S(1)}, u32[]{:S(2)}) copy-start(bf16[512,256]{1,0:T(8,128)(2,1)S(1)} %collective-permute-done.refs_1_) | copy-start | bytes 786436
  96.9 4.9 %copy-start.7 = (bf16[320,512]{1,0:T(8,128)(2,1)}, bf16[320,512]{1,0:T(8,128)(2,1)S(1)}, u32[]{:S(2)}) copy-start(bf16[320,512]{1,0:T(8,128)(2,1)S(1)} %collective-permute-done.2.refs_6_) | copy-start | bytes 983044
  101.8 0.7 copy-start.8
  224.1 41.7 %collective-permute-start.5 = (bf16[320,512]{1,0:T(8,128)(2,1)}, bf16[320,512]{1,0:T(8,128)(2,1)S(1)}, u32[]{:S(2)}, u32[]{:S(2)}) collective-permute-start(bf16[320,512]{1,0:T(8,128)(2,1)} %get-tuple-element.136), channel_id=1, source_target_pairs={{0,16},{8,24},{16,0},{24,8},{1,17},{9,25},{17,1},{25,9},{2,18},{10... | collective-permute-start | bytes 983048 | tf_op jit(solution)/shard_map/ppermute | solution.py:67
  224.2 41.6 %collective-permute-start.6 = (bf16[320,512]{1,0:T(8,128)(2,1)}, bf16[320,512]{1,0:T(8,128)(2,1)S(1)}, u32[]{:S(2)}, u32[]{:S(2)}) collective-permute-start(bf16[320,512]{1,0:T(8,128)(2,1)} %get-tuple-element.137), channel_id=1, source_target_pairs={{0,24},{8,16},{16,8},{24,0},{1,25},{9,17},{17,9},{25,1},{2,26},{10... | collective-permute-start | bytes 983048 | tf_op jit(solution)/shard_map/ppermute | solution.py:67
  227.7 38.2 %collective-permute-start.4 = (bf16[2,320,512]{2,1,0:T(8,128)(2,1)}, bf16[2,320,512]{2,1,0:T(8,128)(2,1)S(1)}, u32[]{:S(2)}, u32[]{:S(2)}) collective-permute-start(bf16[2,320,512]{2,1,0:T(8,128)(2,1)} %get-tuple-element.135), channel_id=1, source_target_pairs={{0,1},{1,0},{2,3},{3,2},{4,5},{5,4},{6,7},{7,6},{8,9},{9,8},{10,11... | collective-permute-start | bytes 1966088 | tf_op jit(solution)/shard_map/ppermute | solution.py:67
  228.1 37.8 %collective-permute-start.3 = (bf16[2,256,1408]{2,1,0:T(8,128)(2,1)}, bf16[2,256,1408]{2,1,0:T(8,128)(2,1)S(1)}, u32[]{:S(2)}, u32[]{:S(2)}) collective-permute-start(bf16[2,256,1408]{2,1,0:T(8,128)(2,1)} %get-tuple-element.134), channel_id=1, source_target_pairs={{0,4},{2,6},{4,0},{6,2},{1,5},{3,7},{5,1},{7,3},{8,12},{10,14},{12... | collective-permute-start | bytes 4325384 | tf_op jit(solution)/shard_map/ppermute | solution.py:67
  265.8 0.7 copy-start.5
  265.9 0.8 copy-start.6
  265.9 1.0 copy-start.4
  265.9 72.1 %copy-start.3 = (bf16[2,256,1408]{2,1,0:T(8,128)(2,1)}, bf16[2,256,1408]{2,1,0:T(8,128)(2,1)S(1)}, u32[]{:S(2)}) copy-start(bf16[2,256,1408]{2,1,0:T(8,128)(2,1)S(1)} %collective-permute-done.3.refs_5_) | copy-start | bytes 4325380
  345.9 3.3 copy-start.1
  349.2 2.3 copy-start
